TPU v7x, 32 devices: a whole 2x2x4 slice. The times are simulated.
32 devices in a mesh: bead: 8 (over z, x), slab: 2 (over y), grp: 2 (over core).
Axes of the slice: x: 2, y: 2, z: 4, core: 2. Of those that a mesh axis runs over, the one named last changes fastest.
Arguments:
- positions: float32 [64, 3, 16384], P('bead', None, ('slab', 'grp')), may hold values from -6 to 6
- momenta: float32 [64, 3, 16384], P('bead', None, ('slab', 'grp')), may hold values from -12 to 12
- force_old: float32 [64, 3, 16384], P('bead', None, ('slab', 'grp')), may hold values from -6 to 6
- noise: float32 [64, 3, 16384], P('bead', None, ('slab', 'grp')), may hold values from -6 to 6
- mass: float32 [16384], P(('slab', 'grp')), may hold values from 1 to 16
- pair_list: int32 [16384, 32], P(('slab', 'grp')), may hold values from 0 to 4351, as said below
- desc_w: bfloat16 [128, 1600], replicated, may hold values from -0.5 to 0.5
- hidden_one: bfloat16 [1600, 240], replicated, may hold values from -0.15625 to 0.15625
- hidden_two: bfloat16 [240, 240], replicated, may hold values from -0.375 to 0.375
- hidden_three: bfloat16 [240, 240], replicated, may hold values from -0.375 to 0.375
- out_w: bfloat16 [240, 3], replicated, may hold values from -0.375 to 0.375
Outputs:
- new_positions: float32 [64, 3, 16384], P('bead', None, ('slab', 'grp'))
- new_momenta: float32 [64, 3, 16384], P('bead', None, ('slab', 'grp'))
- force_new: float32 [64, 3, 16384], P('bead', None, ('slab', 'grp'))
Inputs may be any that keep to these rules, and one draw needn't show every extreme that they name: `pair_list`: for the atom with index li in its slab, every entry lies in li .. li + 256; entries past a count of 16 to 32 per atom name the atom itself, li + 128.
All inputs are finite; a program needn't handle non-finite values.
Results may differ from a plain program's by a relative error of at most 0.00096.
Values sent between devices are 32-bit elements; how exact they have to be, the bound alone decides.
No kernel may reach another device: no remote copies, remote signals or barrier semaphores. Data moves between devices by JAX's collectives and lax.ppermute only.
A program may use at most 128 MiB of HBM per device.

v0:
```python
import math

import jax
import jax.numpy as jnp
import numpy as np
from jax import lax
from jax.experimental import pallas as pl
from jax.experimental.pallas import tpu as pltpu
from jax.sharding import PartitionSpec as P

BEADS = 64
NC = 8
EDGE = 128
LANES = 128

TIME_STEP = 0.1
CYCLE_FREQ = 5.0
CENTROID_FRICTION = 1.0
PAIR_STRENGTH = 0.5

BEST = lax.Precision.HIGHEST


def step_tables():
    b = np.arange(BEADS, dtype=np.float64)
    k = np.arange(BEADS)
    angle = 2.0 * np.pi * ((b[:, None] * b[None, :]) % BEADS) / BEADS
    half = BEADS // 2
    basis = np.where(
        k == 0,
        1.0 / math.sqrt(BEADS),
        np.where(
            k < half,
            math.sqrt(2.0 / BEADS) * np.cos(angle),
            np.where(
                k == half, np.cos(angle) / math.sqrt(BEADS), math.sqrt(2.0 / BEADS) * np.sin(angle)
            ),
        ),
    )
    freq = 2.0 * CYCLE_FREQ * np.sin(np.pi * b / BEADS)
    spacing = b[None, :] / BEADS - np.arange(NC, dtype=np.float64)[:, None] / NC
    kernel = np.ones_like(spacing)
    for order in range(1, NC // 2):
        kernel = kernel + 2.0 * np.cos(2.0 * np.pi * order * spacing)
    kernel = kernel + np.cos(np.pi * NC * spacing)
    contract = kernel / BEADS

    h = 0.5 * TIME_STEP
    safe = np.where(freq > 0.0, freq, 1.0)
    qq = np.where(freq > 0.0, np.cos(safe * h), 1.0)
    qp = np.where(freq > 0.0, np.sin(safe * h) / safe, h)
    pq = np.where(freq > 0.0, -safe * np.sin(safe * h), 0.0)
    pp = qq
    keep = np.exp(-np.where(freq > 0.0, 2.0 * freq, CENTROID_FRICTION) * TIME_STEP)
    kick = np.sqrt(1.0 - keep * keep)
    full_qq = qq * qq + qp * keep * pq
    full_qp = qq * qp + qp * keep * pp
    full_qn = qp * kick
    full_pq = pq * qq + pp * keep * pq
    full_pp = pq * qp + pp * keep * pp
    full_pn = pp * kick
    q_rows = np.concatenate(
        [(basis * full_qq) @ basis.T, (basis * full_qp) @ basis.T, basis * full_qn], axis=1
    )
    p_rows = np.concatenate(
        [(basis * full_pq) @ basis.T, (basis * full_pp) @ basis.T, basis * full_pn], axis=1
    )
    c_rows = contract @ q_rows
    step = np.concatenate([c_rows, q_rows, p_rows], axis=0)
    return step.astype(np.float32), contract.astype(np.float32)


def whole_vmem():
    return pl.BlockSpec(memory_space=pltpu.VMEM)


def params(mebibytes=48):
    return pltpu.CompilerParams(vmem_limit_bytes=mebibytes * 1024 * 1024)


def smem():
    return pl.BlockSpec(memory_space=pltpu.SMEM)


def block_of(place_ref, r, rows):
    return pl.ds(pl.multiple_of((place_ref[0] ^ r) * rows, LANES), rows)


def exchange(blocks, axis):
    count = len(blocks)
    return [blocks[0]] + [
        lax.ppermute(blocks[r], axis, [(i, i ^ r) for i in range(count)]) for r in range(1, count)
    ]


def pack(place, positions, momenta, force_old, noise, groups):
    _, beads, atoms = positions.shape
    rows = atoms // groups

    def kernel(place_ref, q_ref, p_ref, f_ref, n_ref, *rest):
        outs, (p_buf, f_buf, sems) = rest[:groups], rest[groups:]
        loads = [
            pltpu.make_async_copy(p_ref, p_buf, sems.at[0]),
            pltpu.make_async_copy(f_ref, f_buf, sems.at[1]),
        ]
        for r in range(groups):
            at = block_of(place_ref, r, rows)
            for slot, (ref, first) in enumerate(((q_ref, 0), (n_ref, 6))):
                loads.append(
                    pltpu.make_async_copy(
                        ref.at[:, :, at], outs[r].at[pl.ds(first, 3)], sems.at[2 + 2 * r + slot]
                    )
                )
        for load in loads:
            load.start()
        loads[0].wait()
        loads[1].wait()
        for r in range(groups):
            at = block_of(place_ref, r, rows)
            for x in range(3):
                outs[r][3 + x] = p_buf[x, :, at] + 0.5 * TIME_STEP * f_buf[x, :, at]
        for load in loads[2:]:
            load.wait()

    return pl.pallas_call(
        kernel,
        out_shape=[jax.ShapeDtypeStruct((9, beads, rows), jnp.float32)] * groups,
        in_specs=[smem()] + [pl.BlockSpec(memory_space=pltpu.HBM)] * 4,
        out_specs=[whole_vmem()] * groups,
        scratch_shapes=[
            pltpu.VMEM((3, beads, atoms), jnp.float32),
            pltpu.VMEM((3, beads, atoms), jnp.float32),
            pltpu.SemaphoreType.DMA((2 + 2 * groups,)),
        ],
        compiler_params=params(60),
        name="pack",
    )(place, positions, momenta, force_old, noise)


def prepare(pair_list, mass, desc_w, hidden_one, place, rows):
    entries, atoms = pair_list.shape
    desc, env = desc_w.shape
    hid = hidden_one.shape[0]
    order = np.arange(env)
    order = (order % entries) * (env // entries) + order // entries
    permute = jnp.asarray(np.eye(env)[order], jnp.bfloat16)

    def kernel(place_ref, list_ref, mass_ref, w0_ref, w1_ref, order_ref, lists, own, masses, w0, w1):
        for t in range(atoms // LANES):
            at = pl.ds(t * LANES, LANES)
            lists[:, at] = list_ref[:, at] - t * LANES
        block = pl.ds(pl.multiple_of(place_ref[0] * rows, LANES), rows)
        own[...] = lists[:, block]
        masses[...] = mass_ref[:, block]
        w0[...] = lax.dot_general(
            order_ref[...],
            w0_ref[...],
            (((1,), (1,)), ((), ())),
            preferred_element_type=jnp.float32,
        ).astype(w0.dtype)
        w1[...] = w1_ref[...].astype(jnp.float32).T.astype(w1.dtype)

    return pl.pallas_call(
        kernel,
        out_shape=(
            jax.ShapeDtypeStruct((entries, atoms), jnp.int32),
            jax.ShapeDtypeStruct((entries, rows), jnp.int32),
            jax.ShapeDtypeStruct((1, rows), jnp.float32),
            jax.ShapeDtypeStruct((env, desc), jnp.bfloat16),
            jax.ShapeDtypeStruct((desc, hid), jnp.bfloat16),
        ),
        in_specs=[pl.BlockSpec(memory_space=pltpu.SMEM)] + [whole_vmem()] * 5,
        out_specs=(whole_vmem(),) * 5,
        compiler_params=params(),
        cost_estimate=pl.CostEstimate(
            flops=1_000_000_000, bytes_accessed=4_000_000, transcendentals=0
        ),
        name="prepare",
    )(place, pair_list, mass, desc_w, hidden_one, permute)


def contract(place, received, masses, table):
    groups = len(received)
    _, beads, rows = received[0].shape

    def kernel(place_ref, mass_ref, table_ref, own_ref, *rest):
        ins, (c_ref, first, last, fields, own, sem) = rest[: groups - 1], rest[groups - 1 :]

        load = pltpu.make_async_copy(own_ref, own, sem)
        load.start()
        mass = mass_ref[...]
        inverse = 1.0 / mass
        root = lax.rsqrt(mass)

        def scale(g, block):
            for x in range(3):
                fields[x, 0, g] = block[x]
                fields[x, 1, g] = block[3 + x] * inverse
                fields[x, 2, g] = block[6 + x] * root

        for r in range(1, groups):
            scale(place_ref[0] ^ r, ins[r - 1])
        load.wait()
        scale(place_ref[0], own)
        for x in range(3):
            out = jnp.dot(
                table_ref[...],
                fields[x].reshape(3 * BEADS, rows),
                precision=BEST,
                preferred_element_type=jnp.float32,
            )
            c_ref[x] = out
            first[x] = out[:, :EDGE]
            last[x] = out[:, rows - EDGE :]

    edge = jax.ShapeDtypeStruct((3, NC, EDGE), jnp.float32)
    return pl.pallas_call(
        kernel,
        out_shape=(
            jax.ShapeDtypeStruct((3, NC, rows), jnp.float32),
            edge,
            edge,
            jax.ShapeDtypeStruct((3, 3, groups, beads, rows), jnp.float32),
        ),
        in_specs=[smem()]
        + [whole_vmem()] * 2
        + [pl.BlockSpec(memory_space=pltpu.HBM)]
        + [whole_vmem()] * (groups - 1),
        out_specs=(whole_vmem(),) * 4,
        scratch_shapes=[pltpu.VMEM((9, beads, rows), jnp.float32), pltpu.SemaphoreType.DMA],
        compiler_params=params(),
        name="contract",
    )(place, masses, table, *received)


def transform(fields, masses, table):
    _, _, groups, beads, rows = fields.shape

    def kernel(fields_ref, mass_ref, table_ref, out_ref, news, sems):
        mass = mass_ref[...]
        copies = []
        for x in range(3):
            out = jnp.dot(
                table_ref[...],
                fields_ref[x].reshape(3 * BEADS, rows),
                precision=BEST,
                preferred_element_type=jnp.float32,
            )
            news[x] = out[:BEADS].reshape(groups, beads, rows)
            news[3 + x] = (out[BEADS:] * mass).reshape(groups, beads, rows)
            for row in (x, 3 + x):
                copy = pltpu.make_async_copy(news.at[row], out_ref.at[:, row], sems.at[row])
                copy.start()
                copies.append(copy)
        for copy in copies:
            copy.wait()

    return pl.pallas_call(
        kernel,
        out_shape=jax.ShapeDtypeStruct((groups, 6, beads, rows), jnp.float32),
        in_specs=[whole_vmem()] * 3,
        out_specs=pl.BlockSpec(memory_space=pltpu.HBM),
        scratch_shapes=[
            pltpu.VMEM((6, groups, beads, rows), jnp.float32),
            pltpu.SemaphoreType.DMA((6,)),
        ],
        compiler_params=params(),
        cost_estimate=pl.CostEstimate(
            flops=1_000_000_000, bytes_accessed=2_000_000, transcendentals=0
        ),
        name="transform",
    )(fields, masses, table)


def inverse_of(value):
    estimate = pl.reciprocal(value, approx=True)
    return estimate * (2.0 - value * estimate)


def banded(windows, lane, low, high):
    below, middle, above = [
        jnp.take_along_axis(w, lane, axis=1, mode="promise_in_bounds") for w in windows
    ]
    return jnp.where(low, below, jnp.where(high, above, middle))


def entries_of(list_ref, e, base):
    place = list_ref[pl.ds(e, 8), pl.ds(base, LANES)]
    return place & (LANES - 1), place < LANES, place >= 2 * LANES


def on_sublanes(row):
    return jnp.broadcast_to(row, (8, LANES))


def env_units(windows, list_ref, base, envs, inputs):
    entries = list_ref.shape[0]
    for e in range(0, entries, 8):
        lane, low, high = entries_of(list_ref, e, base)
        for c in range(NC):
            apart = []
            for x in range(3):
                tiles = windows(c, x)
                apart.append(banded(tiles, lane, low, high) - tiles[1])
            square = apart[0] * apart[0] + apart[1] * apart[1] + apart[2] * apart[2]
            close = inverse_of(1.0 + square)
            for x, value in enumerate(apart + [close]):
                envs[pl.ds(x * entries + e, 8), pl.ds(c * LANES, LANES)] = value
            yield
    for c in range(NC):
        at = pl.ds(c * LANES, LANES)
        inputs[at, :] = envs[:, at].T.astype(jnp.bfloat16)
        yield


def network(inputs_ref, weights, out_ref, base, units, chunk=256):
    w0_ref, w1_ref, w2_ref, w3_ref, wo_ref = weights
    desc = w0_ref.shape[1]
    inputs = inputs_ref[...]
    total = None
    for f in range(0, desc, chunk):
        size = min(chunk, desc - f)
        first = jnp.dot(inputs, w0_ref[:, pl.ds(f, size)], preferred_element_type=jnp.float32)
        first = jnp.tanh(first.astype(jnp.bfloat16))
        part = jnp.dot(first, w1_ref[pl.ds(f, size), :], preferred_element_type=jnp.float32)
        total = part if total is None else total + part
        for _ in range(6):
            next(units, None)
    layer = jnp.tanh(total).astype(jnp.bfloat16)
    for ref in (w2_ref, w3_ref):
        layer = jnp.tanh(jnp.dot(layer, ref[...], preferred_element_type=jnp.float32)).astype(
            jnp.bfloat16
        )
    out = lax.dot_general(
        wo_ref[...], layer, (((1,), (1,)), ((), ())), preferred_element_type=jnp.float32
    )
    for c in range(NC):
        for x in range(3):
            out_ref[x, pl.ds(c, 1), pl.ds(base, LANES)] = out[
                x : x + 1, c * LANES : (c + 1) * LANES
            ]


def neural_scratch(env):
    return [
        pltpu.VMEM((2, env, NC * LANES), jnp.float32),
        pltpu.VMEM((2, NC * LANES, env), jnp.bfloat16),
    ]


def neural(contracted, lower, upper, lists, weights):
    _, _, rows = contracted.shape
    tiles = rows // LANES

    def kernel(
        c_ref, low_ref, up_ref, list_ref, w0, w1, w2, w3, wo, out_ref, envs, inputs
    ):
        def tile(x, c, t):
            if t < 0:
                ref, at = low_ref, 0
            elif t >= tiles:
                ref, at = up_ref, 0
            else:
                ref, at = c_ref, t * LANES
            return on_sublanes(ref[x, pl.ds(c, 1), pl.ds(at, LANES)])

        def units_of(t):
            if t >= tiles:
                return iter(())
            windows = lambda c, x: [tile(x, c, t + v) for v in (-1, 0, 1)]
            slot = t % 2
            return env_units(windows, list_ref, t * LANES, envs.at[slot], inputs.at[slot])

        for _ in units_of(0):
            pass
        for t in range(tiles):
            units = units_of(t + 1)
            network(inputs.at[t % 2], (w0, w1, w2, w3, wo), out_ref, t * LANES, units)
            for _ in units:
                pass

    return pl.pallas_call(
        kernel,
        out_shape=jax.ShapeDtypeStruct((3, NC, rows), jnp.float32),
        in_specs=[whole_vmem()] * 9,
        out_specs=whole_vmem(),
        scratch_shapes=neural_scratch(weights[0].shape[0]),
        compiler_params=params(),
        cost_estimate=pl.CostEstimate(
            flops=12_000_000_000, bytes_accessed=4_000_000, transcendentals=0
        ),
        name="neural",
    )(contracted, lower, upper, lists, *weights)


def add_pairs(sums, e, b, apart, close):
    for x in range(3):
        part = apart[x] * close
        sums[x, b] = part if e == 0 else sums[x, b] + part


def total_of(sums, x):
    total = sums[x, :, 0, :]
    for s in range(1, 8):
        total = total + sums[x, :, s, :]
    return total


def assemble(fields):
    groups, _, beads, rows = fields.shape
    atoms = groups * rows
    half = beads // 2
    top = float(2**15 - 1)

    def kernel(in_ref, newq, words, fixed, unit_ref, rims):
        largest = jnp.zeros((beads, rows), jnp.float32)
        for g in range(groups):
            at = pl.ds(g * rows, rows)
            for x in range(3):
                value = in_ref[g, x]
                newq[x, :, at] = value
                largest = jnp.maximum(largest, jnp.abs(value))
        limit = jnp.maximum(jnp.max(largest, keepdims=True), 1e-30)
        to_fixed = top / limit
        unit_ref[...] = jnp.broadcast_to(limit / (top * 65536.0), (beads, LANES))
        for g in range(groups):
            at = pl.ds(g * rows, rows)
            for x in range(3):
                value = jnp.floor(in_ref[g, x] * to_fixed + 0.5)
                fixed[x, :, at] = value * 65536.0
                value = value.astype(jnp.int32)
                words[x, :, at] = (value[:half] << 16) | (value[half:] & 65535)
        for rim, t in enumerate((0, LANES, atoms - 2 * LANES, atoms - LANES)):
            rims[rim] = newq[:, :, pl.ds(t, LANES)]

    return pl.pallas_call(
        kernel,
        out_shape=(
            jax.ShapeDtypeStruct((3, beads, atoms), jnp.float32),
            jax.ShapeDtypeStruct((3, half, atoms), jnp.int32),
            jax.ShapeDtypeStruct((3, beads, atoms), jnp.float32),
            jax.ShapeDtypeStruct((beads, LANES), jnp.float32),
            jax.ShapeDtypeStruct((4, 3, beads, LANES), jnp.float32),
        ),
        in_specs=[whole_vmem()],
        out_specs=(whole_vmem(),) * 5,
        compiler_params=params(),
        name="assemble",
    )(fields)


def pair_part(words, fixed, unit, lists, begin, end, edges=()):
    _, beads, atoms = fixed.shape
    half = beads // 2
    tiles = atoms // LANES
    entries = lists.shape[0]

    def kernel(words_ref, fixed_ref, unit_ref, list_ref, *rest):
        ends = rest[: len(edges)]
        pair, sums = rest[len(edges)], rest[-1]
        unit_row = unit_ref[...]
        unit_square = on_sublanes(unit_ref[pl.ds(0, 1), :])
        unit_square = unit_square * unit_square

        def edge(out, at, base, near_tiles):
            for e in range(0, entries, 8):
                lane, low, high = entries_of(list_ref, e, base)
                for b in range(beads):
                    apart = []
                    for x in range(3):
                        windows = [on_sublanes(tile[x, pl.ds(b, 1), :]) for tile in near_tiles]
                        apart.append(banded(windows, lane, low, high) - windows[1])
                    square = apart[0] * apart[0] + apart[1] * apart[1] + apart[2] * apart[2]
                    add_pairs(sums, e, b, apart, inverse_of(1.0 + square))
            for x in range(3):
                out[x, :, pl.ds(at, LANES)] = PAIR_STRENGTH * total_of(sums, x)

        @pl.loop(max(begin, 1), min(end, tiles - 1))
        def _(t):
            base = pl.multiple_of(t * LANES, LANES)

            def row(ref, x, b, v):
                return on_sublanes(ref[x, pl.ds(b, 1), pl.ds(base + (v - 1) * LANES, LANES)])

            for e in range(0, entries, 8):
                lane, low, high = entries_of(list_ref, e, base)
                for b in range(half):
                    both = [
                        banded([row(words_ref, x, b, v) for v in range(3)], lane, low, high)
                        for x in range(3)
                    ]
                    for bead, near in ((b, [w & -65536 for w in both]),
                                       (b + half, [w << 16 for w in both])):
                        apart = [
                            near[x].astype(jnp.float32) - row(fixed_ref, x, bead, 1)
                            for x in range(3)
                        ]
                        square = apart[0] * apart[0] + apart[1] * apart[1] + apart[2] * apart[2]
                        close = inverse_of(1.0 + square * unit_square)
                        add_pairs(sums, e, bead, apart, close)
            at = pl.ds(pl.multiple_of((t - begin) * LANES, LANES), LANES)
            for x in range(3):
                pair[x, :, at] = (PAIR_STRENGTH * unit_row) * total_of(sums, x)

        if edges:
            rims, lower, upper = ends
            last = (tiles - 1) * LANES
            edge(rest[len(edges) + 1], 0, 0, [lower, rims.at[0], rims.at[1]])
            edge(pair, last - begin * LANES, last, [rims.at[2], rims.at[3], upper])

    out_shape = [jax.ShapeDtypeStruct((3, beads, (end - begin) * LANES), jnp.float32)]
    if edges:
        out_shape.append(jax.ShapeDtypeStruct((3, beads, LANES), jnp.float32))
    return pl.pallas_call(
        kernel,
        out_shape=out_shape,
        in_specs=[whole_vmem()] * (4 + len(edges)),
        out_specs=[whole_vmem()] * len(out_shape),
        scratch_shapes=[pltpu.VMEM((3, beads, 8, LANES), jnp.float32)],
        compiler_params=params(),
        cost_estimate=pl.CostEstimate(
            flops=300_000_000 * (end - begin), bytes_accessed=2_000_000, transcendentals=0
        ),
        name=f"pair_{begin}",
    )(words, fixed, unit, lists, *edges)


def finish(place, pairs, first, fields, neural_parts, partners, coefs):
    groups, _, beads, size = fields[0].shape
    rows = size * len(fields)
    atoms = groups * rows
    counts = [part.shape[0] for part in neural_parts]

    def kernel(place_ref, first_ref, coef_ref, *rest):
        halves, rest = rest[: len(pairs)], rest[len(pairs) :]
        ins, rest = rest[: len(fields)], rest[len(fields) :]
        blocks, (newp, newf) = rest[: len(counts)], rest[len(counts) :]
        own = place_ref[0]
        at = 0
        for half in halves:
            newf[:, :, pl.ds(at, half.shape[2])] = half[...]
            at += half.shape[2]
        newf[:, :, pl.ds(0, LANES)] = first_ref[...]
        coef = [coef_ref[c, own] for c in range(NC)]
        blocks = [block.at[i] for block, count in zip(blocks, counts) for i in range(count)]
        for r, block in zip(partners, blocks):
            g = own ^ r
            for t in range(0, rows, LANES):
                at = pl.ds(pl.multiple_of(g * rows + t, LANES), LANES)
                moved = ins[t // size].at[g, :, :, pl.ds(t % size, LANES)]
                for x in range(3):
                    force = newf[x, :, at]
                    for c in range(NC):
                        force = force + coef[c] * block[x, pl.ds(c, 1), pl.ds(t, LANES)]
                    newf[x, :, at] = force
                    newp[x, :, at] = moved[3 + x] + 0.5 * TIME_STEP * force

    out = jax.ShapeDtypeStruct((3, beads, atoms), jnp.float32)
    return pl.pallas_call(
        kernel,
        out_shape=(out,) * 2,
        in_specs=[smem()]
        + [whole_vmem()] * (2 + len(pairs) + len(fields) + len(neural_parts)),
        out_specs=(whole_vmem(),) * 2,
        compiler_params=params(),
        name="finish",
    )(place, first, coefs, *pairs, *fields, *neural_parts)


def doubling_step(have, partners, axis, bit):
    count = lax.axis_size(axis)
    got = lax.ppermute(have, axis, [(i, i ^ bit) for i in range(count)])
    return got, partners + [r ^ bit for r in partners]


def body(
    positions,
    momenta,
    force_old,
    noise,
    mass,
    pair_list,
    desc_w,
    hidden_one,
    hidden_two,
    hidden_three,
    out_w,
):
    beads, _, atoms = positions.shape
    groups = lax.axis_size("bead")
    slabs = lax.axis_size(("slab", "grp"))
    rows = atoms // groups
    place = lax.axis_index("bead").astype(jnp.int32)[None]
    step, kernel = step_tables()

    swap = lambda field: jnp.transpose(field, (1, 0, 2))
    sends = pack(place, swap(positions), swap(momenta), swap(force_old), swap(noise), groups)
    received = exchange(sends, "bead")

    lists, block_lists, masses, env_w, w1 = prepare(
        pair_list.T, mass[None, :], desc_w.T, hidden_one.T, place, rows
    )
    received, lists, block_lists, masses, env_w, w1 = lax.optimization_barrier(
        (received, lists, block_lists, masses, env_w, w1)
    )
    weights = (env_w, w1, hidden_two, hidden_three, out_w.T)

    contracted, first, last, scaled = contract(place, received, masses, jnp.asarray(step[:NC]))
    ring = [
        (g * slabs + s, ((g + 1) % groups) * slabs + (s + (g + 1) // groups) % slabs)
        for g in range(groups)
        for s in range(slabs)
    ]
    back = [(j, i) for i, j in ring]
    every = ("bead", "slab", "grp")
    lower = lax.ppermute(last, every, ring)
    upper = lax.ppermute(first, every, back)
    returns = transform(scaled, masses, jnp.asarray(step[NC:]))
    returns, lower, upper = lax.optimization_barrier((returns, lower, upper))
    fields = lax.all_to_all(returns, "bead", split_axis=0, concat_axis=0, tiled=True)

    forces = neural(contracted, lower, upper, block_lists, weights)
    bits = [1 << i for i in range(groups.bit_length() - 2, -1, -1)]
    have = forces[None]
    got, partners = doubling_step(have, [0], "bead", bits[0])
    fields, forces = lax.optimization_barrier((fields, forces))

    new_q, words, fixed, unit, rims = assemble(fields)
    slab_ring = [(s, (s + 1) % slabs) for s in range(slabs)]
    slab_back = [(j, i) for i, j in slab_ring]
    q_lower = lax.ppermute(rims[3], ("slab", "grp"), slab_ring)
    q_upper = lax.ppermute(rims[0], ("slab", "grp"), slab_back)

    words, got = lax.optimization_barrier((words, got))
    tiles = atoms // LANES
    cut = 3 * tiles // 8
    for bit in bits[1:2]:
        have = jnp.concatenate([have, got], axis=0)
        got, partners = doubling_step(have, partners, "bead", bit)
    pairs = pair_part(words, fixed, unit, lists, 0, cut)
    words, pairs, got = lax.optimization_barrier((words, pairs, got))
    for bit in bits[2:]:
        have = jnp.concatenate([have, got], axis=0)
        got, partners = doubling_step(have, partners, "bead", bit)
    rest, first = pair_part(
        words, fixed, unit, lists, cut, tiles, (rims, q_lower, q_upper)
    )

    coefs = (kernel * np.float32(BEADS / NC)).reshape(NC, groups, beads, 1)
    coefs = jnp.asarray(np.broadcast_to(coefs, (NC, groups, beads, LANES)))
    new_p, force = finish(
        place, [*pairs, rest], first, [fields], (have, got), partners, coefs
    )
    return tuple(swap(out) for out in (new_q, new_p, force))


def solution(mesh):
    field = P("bead", None, ("slab", "grp"))
    placed = (field,) * 4 + (P(("slab", "grp")), P(("slab", "grp"), None)) + (P(),) * 5
    return jax.shard_map(
        body, mesh=mesh, in_specs=placed, out_specs=(field,) * 3, check_vma=False
    )
```

profile of v0, /device:TPU:0, one launch (start us, length us, event | category | flops | bytes accessed | tf_op | source)
XLA Modules:
  0.0 84.5 jit_solution(6159690729976392864)
XLA Ops:
  0.6 0.0 copy-start.10
  0.7 2.5 %pack.1 = (f32[9,8,512]{2,1,0:T(8,128)}, f32[9,8,512]{2,1,0:T(8,128)}, f32[9,8,512]{2,1,0:T(8,128)}, f32[9,8,512]{2,1,0:T(8,128)}, f32[9,8,512]{2,1,0:T(8,128)},...) custom-call(s32[1]{0:T(128)} %bitcast.place_ref, f32[3,8,4096]{2,1,0:T(8,128)} %bitcast.26, ...), custom_call_target="tpu_custom_call" | custom-call | tf_op jit(solution)/shard_map/pack/pallas_call | solution.py:125
  3.2 3.0 %collective-permute-start = (f32[9,8,512]{2,1,0:T(8,128)}, f32[9,8,512]{2,1,0:T(8,128)S(1)}, u32[]{:S(2)}, u32[]{:S(2)}) collective-permute-start(f32[9,8,512]{2,1,0:T(8,128)} %get-tuple-element.52), channel_id=1, source_target_pairs={{0,4},{4,0},{8,12},{12,8},{16,20},{20,16},{24,28},{28,24},{1,5},{5... | collective-permute-start | bytes 442376 | tf_op jit(solution)/shard_map/ppermute | solution.py:92
  6.2 1.6 %collective-permute-start.1 = (f32[9,8,512]{2,1,0:T(8,128)}, f32[9,8,512]{2,1,0:T(8,128)S(1)}, u32[]{:S(2)}, u32[]{:S(2)}) collective-permute-start(f32[9,8,512]{2,1,0:T(8,128)} %get-tuple-element.53), channel_id=1, source_target_pairs={{0,8},{4,12},{8,0},{12,4},{16,24},{20,28},{24,16},{28,20},{1,9},{5... | collective-permute-start | bytes 442376 | tf_op jit(solution)/shard_map/ppermute | solution.py:92
  7.8 0.0 collective-permute-start.2
  7.8 3.0 %collective-permute-start.3 = (f32[9,8,512]{2,1,0:T(8,128)}, f32[9,8,512]{2,1,0:T(8,128)S(1)}, u32[]{:S(2)}, u32[]{:S(2)}) collective-permute-start(f32[9,8,512]{2,1,0:T(8,128)} %get-tuple-element.55), channel_id=1, source_target_pairs={{0,16},{4,20},{8,24},{12,28},{16,0},{20,4},{24,8},{28,12},{1,17},{... | collective-permute-start | bytes 442376 | tf_op jit(solution)/shard_map/ppermute | solution.py:92
  10.8 1.3 %collective-permute-start.4 = (f32[9,8,512]{2,1,0:T(8,128)}, f32[9,8,512]{2,1,0:T(8,128)S(1)}, u32[]{:S(2)}, u32[]{:S(2)}) collective-permute-start(f32[9,8,512]{2,1,0:T(8,128)} %get-tuple-element.56), channel_id=1, source_target_pairs={{0,20},{4,16},{8,28},{12,24},{16,4},{20,0},{24,12},{28,8},{1,21},{... | collective-permute-start | bytes 442376 | tf_op jit(solution)/shard_map/ppermute | solution.py:92
  12.1 0.0 collective-permute-done.rest_0_
  12.1 3.6 %collective-permute-start.5 = (f32[9,8,512]{2,1,0:T(8,128)}, f32[9,8,512]{2,1,0:T(8,128)S(1)}, u32[]{:S(2)}, u32[]{:S(2)}) collective-permute-start(f32[9,8,512]{2,1,0:T(8,128)} %get-tuple-element.57), channel_id=1, source_target_pairs={{0,24},{4,28},{8,16},{12,20},{16,8},{20,12},{24,0},{28,4},{1,25},{... | collective-permute-start | bytes 442376 | tf_op jit(solution)/shard_map/ppermute | solution.py:92
  15.7 2.7 %collective-permute-done.1.rest_1_ = f32[9,8,512]{2,1,0:T(8,128)S(1)} collective-permute-done((f32[9,8,512]{2,1,0:T(8,128)}, f32[9,8,512]{2,1,0:T(8,128)S(1)}, u32[]{:S(2)}, u32[]{:S(2)}) %collective-permute-start.1) | collective-permute-done | bytes 147488 | tf_op jit(solution)/shard_map/ppermute | solution.py:92
  18.4 0.9 %collective-permute-start.6 = (f32[9,8,512]{2,1,0:T(8,128)}, f32[9,8,512]{2,1,0:T(8,128)S(1)}, u32[]{:S(2)}, u32[]{:S(2)}) collective-permute-start(f32[9,8,512]{2,1,0:T(8,128)} %get-tuple-element.58), channel_id=1, source_target_pairs={{0,28},{4,24},{8,20},{12,16},{16,12},{20,8},{24,4},{28,0},{1,29},{... | collective-permute-start | bytes 442376 | tf_op jit(solution)/shard_map/ppermute | solution.py:92
  19.4 0.0 copy-start.4
  19.4 1.0 %copy-done.4 = bf16[128,1600]{0,1:T(8,128)(2,1)S(1)} copy-done((bf16[128,1600]{0,1:T(8,128)(2,1)S(1)}, bf16[128,1600]{0,1:T(8,128)(2,1)}, u32[]{:S(2)}) %copy-start.4) | copy-done | bytes 409624
  20.4 0.4 prepare.1
  20.7 0.0 copy-start.9
  20.7 0.0 collective-permute-done.2.rest_2_
  20.8 0.0 collective-permute-done.3.rest_3_
  20.8 11.7 %collective-permute-done.4.rest_4_ = f32[9,8,512]{2,1,0:T(8,128)S(1)} collective-permute-done((f32[9,8,512]{2,1,0:T(8,128)}, f32[9,8,512]{2,1,0:T(8,128)S(1)}, u32[]{:S(2)}, u32[]{:S(2)}) %collective-permute-start.4) | collective-permute-done | bytes 147488 | tf_op jit(solution)/shard_map/ppermute | solution.py:92
  32.5 0.0 collective-permute-done.5.rest_5_
  32.5 0.0 collective-permute-done.6.rest_6_
  32.5 0.9 %contract.1 = (f32[3,8,512]{2,1,0:T(8,128)S(1)}, f32[3,8,128]{2,1,0:T(8,128)S(1)}, f32[3,8,128]{2,1,0:T(8,128)S(1)}, f32[3,3,8,8,512]{4,3,2,1,0:T(8,128)S(1)}) custom-call(s32[1]{0:T(128)} %bitcast.place_ref, f32[1,512]{1,0:T(1,128)S(1)} %get-tuple-element.64.mass_ref, f32[8,192]{1,0:T(8,128)S(1)} %copy-done.1, f32[9,8,512]{2,1,0:T(8,128)S(1)} %copy-done, ...), custom_call_target="tpu_custom_call" | custom-call | tf_op jit(solution)/shard_map/contract/pallas_call | solution.py:217
  33.5 0.8 %collective-permute-start.7 = (f32[3,8,128]{2,1,0:T(8,128)S(1)}, f32[3,8,128]{2,1,0:T(8,128)S(1)}, u32[]{:S(2)}, u32[]{:S(2)}) collective-permute-start(f32[3,8,128]{2,1,0:T(8,128)S(1)} %get-tuple-element.74), channel_id=1, source_target_pairs={{0,4},{1,5},{2,6},{3,7},{4,8},{5,9},{6,10},{7,11},{8,12},{9,13},{1... | collective-permute-start | bytes 36872 | tf_op jit(solution)/shard_map/ppermute | solution.py:616
  34.3 4.6 %collective-permute-start.8 = (f32[3,8,128]{2,1,0:T(8,128)S(1)}, f32[3,8,128]{2,1,0:T(8,128)S(1)}, u32[]{:S(2)}, u32[]{:S(2)}) collective-permute-start(f32[3,8,128]{2,1,0:T(8,128)S(1)} %get-tuple-element.75), channel_id=1, source_target_pairs={{4,0},{5,1},{6,2},{7,3},{8,4},{9,5},{10,6},{11,7},{12,8},{13,9},{1... | collective-permute-start | bytes 36872 | tf_op jit(solution)/shard_map/ppermute | solution.py:617
  38.9 1.6 %transform.1 = f32[8,6,8,512]{3,2,1,0:T(8,128)} custom-call(f32[3,3,8,8,512]{4,3,2,1,0:T(8,128)S(1)} %get-tuple-element.73.fields_ref, f32[1,512]{1,0:T(1,128)S(1)} %get-tuple-element.64.mass_ref, f32[128,192]{1,0:T(8,128)S(1)} %copy-done.9), custom_call_target="tpu_custom_call" | custom-call | flops 1000000000 | bytes 2000000 | tf_op jit(solution)/shard_map/transform/pallas_call | solution.py:258
  40.5 0.0 copy-start.5
  40.5 0.0 copy-start.6
  40.5 0.0 copy-start.8
  40.5 0.0 collective-permute-done.7.low_ref
  40.5 1.7 %collective-permute-done.8.up_ref = f32[3,8,128]{2,1,0:T(8,128)S(1)} collective-permute-done((f32[3,8,128]{2,1,0:T(8,128)S(1)}, f32[3,8,128]{2,1,0:T(8,128)S(1)}, u32[]{:S(2)}, u32[]{:S(2)}) %collective-permute-start.8) | collective-permute-done | bytes 12320 | tf_op jit(solution)/shard_map/ppermute | solution.py:617
  42.2 6.0 %all-to-all-start = ((f32[8,6,8,512]{3,2,1,0:T(8,128)}), f32[8,6,8,512]{3,2,1,0:T(8,128)S(1)}, u32[]{:S(2)}, u32[]{:S(2)}) async-start(f32[8,6,8,512]{3,2,1,0:T(8,128)} %transform.1), calls=%async_computation | async-start | bytes 1572864 | tf_op jit(solution)/shard_map/all_to_all | solution.py:620
  48.2 11.5 %neural.1 = f32[3,8,512]{2,1,0:T(8,128)S(1)} custom-call(f32[3,8,512]{2,1,0:T(8,128)S(1)} %get-tuple-element.77.c_ref, f32[3,8,128]{2,1,0:T(8,128)S(1)} %collective-permute-done.7.low_ref, f32[3,8,128]{2,1,0:T(8,128)S(1)} %collective-permute-done.8.up_ref, s32[32,512]{1,0:T(8,128)S(1)} %get-tuple-element.80.list_ref, ...), custom_call_target="tpu_custom_call" | custom-call | flops 12000000000 | bytes 4000000 | tf_op jit(solution)/shard_map/neural/pallas_call | solution.py:382
  59.8 2.9 %collective-permute-start.9 = (f32[1,3,8,512]{3,2,1,0:T(8,128)S(1)}, f32[1,3,8,512]{3,2,1,0:T(8,128)S(1)}, u32[]{:S(2)}, u32[]{:S(2)}) collective-permute-start(f32[1,3,8,512]{3,2,1,0:T(8,128)S(1)} %bitcast.18), channel_id=1, source_target_pairs={{0,16},{4,20},{8,24},{12,28},{16,0},{20,4},{24,8},{28,12},{1,17},{... | collective-permute-start | bytes 147464 | tf_op jit(solution)/shard_map/ppermute | solution.py:572
  62.7 6.6 %all-to-all-done.in_ref.rest_2_ = f32[8,6,8,512]{3,2,1,0:T(8,128)S(1)} async-done(((f32[8,6,8,512]{3,2,1,0:T(8,128)}), f32[8,6,8,512]{3,2,1,0:T(8,128)S(1)}, u32[]{:S(2)}, u32[]{:S(2)}) %all-to-all-start) | async-done | bytes 786464 | tf_op jit(solution)/shard_map/all_to_all | solution.py:620
  69.3 0.8 assemble.1
  70.1 0.0 collective-permute-done.9
  70.1 0.1 collective-permute-start.10
  70.2 0.1 collective-permute-start.11
  70.2 1.7 %collective-permute-start.12 = (f32[3,8,128]{2,1,0:T(8,128)S(1)}, f32[3,8,128]{2,1,0:T(8,128)S(1)}, u32[]{:S(2)}, u32[]{:S(2)}) collective-permute-start(f32[3,8,128]{2,1,0:T(8,128)S(1)} %get-tuple-element.99), channel_id=1, source_target_pairs={{1,0},{2,1},{3,2},{0,3},{5,4},{6,5},{7,6},{4,7},{9,8},{10,9},{11,1... | collective-permute-start | bytes 36872 | tf_op jit(solution)/shard_map/ppermute | solution.py:632
  72.0 3.2 %pair_0.1.rest_0_ = f32[3,8,1536]{2,1,0:T(8,128)S(1)} custom-call(s32[3,4,4096]{2,1,0:T(4,128)S(1)} %get-tuple-element.91.words_ref, f32[3,8,4096]{2,1,0:T(8,128)S(1)} %get-tuple-element.87.fixed_ref, f32[8,128]{1,0:T(8,128)S(1)} %get-tuple-element.88.unit_ref, s32[32,4096]{1,0:T(8,128)S(1)} %get-tuple-element.89.list_ref), custom_call_target="tpu_custom_call" | custom-call | flops 3600000000 | bytes 2000000 | tf_op jit(solution)/shard_map/pair_0/pallas_call | solution.py:514
  75.2 0.0 collective-permute-done.10
  75.2 0.0 copy-start.11
  75.3 1.4 %collective-permute-start.13 = (f32[4,3,8,512]{3,2,1,0:T(8,128)S(1)}, f32[4,3,8,512]{3,2,1,0:T(8,128)S(1)}, u32[]{:S(2)}, u32[]{:S(2)}) collective-permute-start(f32[4,3,8,512]{3,2,1,0:T(8,128)S(1)} %pad_maximum_fusion.rest_3_), channel_id=1, source_target_pairs={{0,4},{4,0},{8,12},{12,8},{16,20},{20,16},{24,28},{28,24},{1,5},{5... | collective-permute-start | bytes 589832 | tf_op jit(solution)/shard_map/ppermute | solution.py:572
  76.7 0.0 collective-permute-done.11.rest_1_
  76.7 0.0 collective-permute-done.12.rest_2_
  76.7 6.3 %pair_12.1 = (f32[3,8,2560]{2,1,0:T(8,128)S(1)}, f32[3,8,128]{2,1,0:T(8,128)S(1)}) custom-call(s32[3,4,4096]{2,1,0:T(4,128)S(1)} %get-tuple-element.91.words_ref, f32[3,8,4096]{2,1,0:T(8,128)S(1)} %get-tuple-element.87.fixed_ref, f32[8,128]{1,0:T(8,128)S(1)} %get-tuple-element.88.unit_ref, s32[32,4096]{1,0:T(8,128)S(1)} %get-tuple-element.89.list_ref, ...), custom_call_target="tpu_custom_call" | custom-call | flops 6000000000 | bytes 2000000 | tf_op jit(solution)/shard_map/pair_12/pallas_call | solution.py:514
  83.0 0.0 collective-permute-done.13.rest_4_
  83.0 0.1 jit_solution_.3.coef_ref
  83.1 1.3 %finish.1 = (f32[3,8,4096]{2,1,0:T(8,128)}, f32[3,8,4096]{2,1,0:T(8,128)}) custom-call(s32[1]{0:T(128)} %bitcast.place_ref, f32[3,8,128]{2,1,0:T(8,128)S(1)} %get-tuple-element.93.first_ref, f32[8,8,8,128]{3,2,1,0:T(8,128)S(1)} %jit_solution_.3.coef_ref, f32[3,8,1536]{2,1,0:T(8,128)S(1)} %pair_0.1.rest_0_, f32[3,8,2560]{2,1,0:T(8,128)S(1)} %get-tuple-element.95.rest_1_, ...), custom_call_target="tpu_custom_call" | custom-call | tf_op jit(solution)/shard_map/finish/pallas_call | solution.py:559
  (19 shorter events, 0.1 us)
Async XLA Ops:
  0.6 18.7 %copy-start.10 = (bf16[128,128]{1,0:T(8,128)(2,1)S(1)}, bf16[128,128]{1,0:T(8,128)(2,1)}, u32[]{:S(2)}) copy-start(bf16[128,128]{1,0:T(8,128)(2,1)} %constant.14.clone.order_ref) | copy-start | bytes 98308
  0.6 18.7 %copy-start.3 = (s32[4096,32]{0,1:T(8,128)S(1)}, s32[4096,32]{0,1:T(8,128)}, u32[]{:S(2)}) copy-start(s32[4096,32]{0,1:T(8,128)} %param.20) | copy-start | bytes 1572868
  0.7 18.7 %copy-start.7 = (f32[4096]{0:T(1024)S(1)}, f32[4096]{0:T(1024)}, u32[]{:S(2)}) copy-start(f32[4096]{0:T(1024)} %param.19) | copy-start | bytes 49156
  0.7 18.7 %copy-start.2 = (bf16[1600,240]{0,1:T(8,128)(2,1)S(1)}, bf16[1600,240]{0,1:T(8,128)(2,1)}, u32[]{:S(2)}) copy-start(bf16[1600,240]{0,1:T(8,128)(2,1)} %param.22) | copy-start | bytes 2304004
  3.2 8.9 %collective-permute-start = (f32[9,8,512]{2,1,0:T(8,128)}, f32[9,8,512]{2,1,0:T(8,128)S(1)}, u32[]{:S(2)}, u32[]{:S(2)}) collective-permute-start(f32[9,8,512]{2,1,0:T(8,128)} %get-tuple-element.52), channel_id=1, source_target_pairs={{0,4},{4,0},{8,12},{12,8},{16,20},{20,16},{24,28},{28,24},{1,5},{5... | collective-permute-start | bytes 442376 | tf_op jit(solution)/shard_map/ppermute | solution.py:92
  6.2 12.2 %collective-permute-start.1 = (f32[9,8,512]{2,1,0:T(8,128)}, f32[9,8,512]{2,1,0:T(8,128)S(1)}, u32[]{:S(2)}, u32[]{:S(2)}) collective-permute-start(f32[9,8,512]{2,1,0:T(8,128)} %get-tuple-element.53), channel_id=1, source_target_pairs={{0,8},{4,12},{8,0},{12,4},{16,24},{20,28},{24,16},{28,20},{1,9},{5... | collective-permute-start | bytes 442376 | tf_op jit(solution)/shard_map/ppermute | solution.py:92
  7.8 12.9 %collective-permute-start.2 = (f32[9,8,512]{2,1,0:T(8,128)}, f32[9,8,512]{2,1,0:T(8,128)S(1)}, u32[]{:S(2)}, u32[]{:S(2)}) collective-permute-start(f32[9,8,512]{2,1,0:T(8,128)} %get-tuple-element.54), channel_id=1, source_target_pairs={{0,12},{4,8},{8,4},{12,0},{16,28},{20,24},{24,20},{28,16},{1,13},{... | collective-permute-start | bytes 442376 | tf_op jit(solution)/shard_map/ppermute | solution.py:92
  7.8 13.0 %collective-permute-start.3 = (f32[9,8,512]{2,1,0:T(8,128)}, f32[9,8,512]{2,1,0:T(8,128)S(1)}, u32[]{:S(2)}, u32[]{:S(2)}) collective-permute-start(f32[9,8,512]{2,1,0:T(8,128)} %get-tuple-element.55), channel_id=1, source_target_pairs={{0,16},{4,20},{8,24},{12,28},{16,0},{20,4},{24,8},{28,12},{1,17},{... | collective-permute-start | bytes 442376 | tf_op jit(solution)/shard_map/ppermute | solution.py:92
  10.8 21.7 %collective-permute-start.4 = (f32[9,8,512]{2,1,0:T(8,128)}, f32[9,8,512]{2,1,0:T(8,128)S(1)}, u32[]{:S(2)}, u32[]{:S(2)}) collective-permute-start(f32[9,8,512]{2,1,0:T(8,128)} %get-tuple-element.56), channel_id=1, source_target_pairs={{0,20},{4,16},{8,28},{12,24},{16,4},{20,0},{24,12},{28,8},{1,21},{... | collective-permute-start | bytes 442376 | tf_op jit(solution)/shard_map/ppermute | solution.py:92
  12.1 20.4 %collective-permute-start.5 = (f32[9,8,512]{2,1,0:T(8,128)}, f32[9,8,512]{2,1,0:T(8,128)S(1)}, u32[]{:S(2)}, u32[]{:S(2)}) collective-permute-start(f32[9,8,512]{2,1,0:T(8,128)} %get-tuple-element.57), channel_id=1, source_target_pairs={{0,24},{4,28},{8,16},{12,20},{16,8},{20,12},{24,0},{28,4},{1,25},{... | collective-permute-start | bytes 442376 | tf_op jit(solution)/shard_map/ppermute | solution.py:92
  18.4 14.1 %collective-permute-start.6 = (f32[9,8,512]{2,1,0:T(8,128)}, f32[9,8,512]{2,1,0:T(8,128)S(1)}, u32[]{:S(2)}, u32[]{:S(2)}) collective-permute-start(f32[9,8,512]{2,1,0:T(8,128)} %get-tuple-element.58), channel_id=1, source_target_pairs={{0,28},{4,24},{8,20},{12,16},{16,12},{20,8},{24,4},{28,0},{1,29},{... | collective-permute-start | bytes 442376 | tf_op jit(solution)/shard_map/ppermute | solution.py:92
  19.4 1.0 %copy-start.4 = (bf16[128,1600]{0,1:T(8,128)(2,1)S(1)}, bf16[128,1600]{0,1:T(8,128)(2,1)}, u32[]{:S(2)}) copy-start(bf16[128,1600]{0,1:T(8,128)(2,1)} %param.21) | copy-start | bytes 1228804
  20.4 12.1 %copy-start = (f32[9,8,512]{2,1,0:T(8,128)S(1)}, f32[9,8,512]{2,1,0:T(8,128)}, u32[]{:S(2)}) copy-start(f32[9,8,512]{2,1,0:T(8,128)} %get-tuple-element.65.own_ref) | copy-start | bytes 442372
  20.4 12.1 %copy-start.1 = (f32[8,192]{1,0:T(8,128)S(1)}, f32[8,192]{1,0:T(8,128)}, u32[]{:S(2)}) copy-start(f32[8,192]{1,0:T(8,128)} %constant.15.clone.table_ref) | copy-start | bytes 18436
  20.7 18.1 %copy-start.9 = (f32[128,192]{1,0:T(8,128)S(1)}, f32[128,192]{1,0:T(8,128)}, u32[]{:S(2)}) copy-start(f32[128,192]{1,0:T(8,128)} %constant.16.clone.table_ref) | copy-start | bytes 294916
  33.5 7.1 %collective-permute-start.7 = (f32[3,8,128]{2,1,0:T(8,128)S(1)}, f32[3,8,128]{2,1,0:T(8,128)S(1)}, u32[]{:S(2)}, u32[]{:S(2)}) collective-permute-start(f32[3,8,128]{2,1,0:T(8,128)S(1)} %get-tuple-element.74), channel_id=1, source_target_pairs={{0,4},{1,5},{2,6},{3,7},{4,8},{5,9},{6,10},{7,11},{8,12},{9,13},{1... | collective-permute-start | bytes 36872 | tf_op jit(solution)/shard_map/ppermute | solution.py:616
  34.3 7.9 %collective-permute-start.8 = (f32[3,8,128]{2,1,0:T(8,128)S(1)}, f32[3,8,128]{2,1,0:T(8,128)S(1)}, u32[]{:S(2)}, u32[]{:S(2)}) collective-permute-start(f32[3,8,128]{2,1,0:T(8,128)S(1)} %get-tuple-element.75), channel_id=1, source_target_pairs={{4,0},{5,1},{6,2},{7,3},{8,4},{9,5},{10,6},{11,7},{12,8},{13,9},{1... | collective-permute-start | bytes 36872 | tf_op jit(solution)/shard_map/ppermute | solution.py:617
  40.5 7.7 %copy-start.5 = (bf16[240,240]{1,0:T(8,128)(2,1)S(1)}, bf16[240,240]{1,0:T(8,128)(2,1)}, u32[]{:S(2)}) copy-start(bf16[240,240]{1,0:T(8,128)(2,1)} %w2.1) | copy-start | bytes 345604
  40.5 7.7 %copy-start.6 = (bf16[240,240]{1,0:T(8,128)(2,1)S(1)}, bf16[240,240]{1,0:T(8,128)(2,1)}, u32[]{:S(2)}) copy-start(bf16[240,240]{1,0:T(8,128)(2,1)} %w3.1) | copy-start | bytes 345604
  40.5 7.7 %copy-start.8 = (bf16[240,3]{0,1:T(4,128)(2,1)S(1)}, bf16[240,3]{0,1:T(4,128)(2,1)}, u32[]{:S(2)}) copy-start(bf16[240,3]{0,1:T(4,128)(2,1)} %param.25) | copy-start | bytes 4324
  42.2 27.1 %all-to-all-start = ((f32[8,6,8,512]{3,2,1,0:T(8,128)}), f32[8,6,8,512]{3,2,1,0:T(8,128)S(1)}, u32[]{:S(2)}, u32[]{:S(2)}) async-start(f32[8,6,8,512]{3,2,1,0:T(8,128)} %transform.1), calls=%async_computation | async-start | bytes 1572864 | tf_op jit(solution)/shard_map/all_to_all | solution.py:620
  59.8 10.3 %collective-permute-start.9 = (f32[1,3,8,512]{3,2,1,0:T(8,128)S(1)}, f32[1,3,8,512]{3,2,1,0:T(8,128)S(1)}, u32[]{:S(2)}, u32[]{:S(2)}) collective-permute-start(f32[1,3,8,512]{3,2,1,0:T(8,128)S(1)} %bitcast.18), channel_id=1, source_target_pairs={{0,16},{4,20},{8,24},{12,28},{16,0},{20,4},{24,8},{28,12},{1,17},{... | collective-permute-start | bytes 147464 | tf_op jit(solution)/shard_map/ppermute | solution.py:572
  70.1 5.1 %collective-permute-start.10 = (f32[2,3,8,512]{3,2,1,0:T(8,128)S(1)}, f32[2,3,8,512]{3,2,1,0:T(8,128)S(1)}, u32[]{:S(2)}, u32[]{:S(2)}) collective-permute-start(f32[2,3,8,512]{3,2,1,0:T(8,128)S(1)} %pad_maximum_fusion.1), channel_id=1, source_target_pairs={{0,8},{4,12},{8,0},{12,4},{16,24},{20,28},{24,16},{28,20},{1,9},{5... | collective-permute-start | bytes 294920 | tf_op jit(solution)/shard_map/ppermute | solution.py:572
  70.2 6.5 %collective-permute-start.11 = (f32[3,8,128]{2,1,0:T(8,128)S(1)}, f32[3,8,128]{2,1,0:T(8,128)S(1)}, u32[]{:S(2)}, u32[]{:S(2)}) collective-permute-start(f32[3,8,128]{2,1,0:T(8,128)S(1)} %get-tuple-element.100), channel_id=1, source_target_pairs={{0,1},{1,2},{2,3},{3,0},{4,5},{5,6},{6,7},{7,4},{8,9},{9,10},{10,1... | collective-permute-start | bytes 36872 | tf_op jit(solution)/shard_map/ppermute | solution.py:631
  70.2 6.4 %collective-permute-start.12 = (f32[3,8,128]{2,1,0:T(8,128)S(1)}, f32[3,8,128]{2,1,0:T(8,128)S(1)}, u32[]{:S(2)}, u32[]{:S(2)}) collective-permute-start(f32[3,8,128]{2,1,0:T(8,128)S(1)} %get-tuple-element.99), channel_id=1, source_target_pairs={{1,0},{2,1},{3,2},{0,3},{5,4},{6,5},{7,6},{4,7},{9,8},{10,9},{11,1... | collective-permute-start | bytes 36872 | tf_op jit(solution)/shard_map/ppermute | solution.py:632
  75.2 7.8 %copy-start.11 = (f32[8,8,8]{2,1,0:T(8,128)S(1)}, f32[8,8,8]{2,1,0:T(8,128)}, u32[]{:S(2)}) copy-start(f32[8,8,8]{2,1,0:T(8,128)} %constant.17.clone) | copy-start | bytes 6148
  75.3 7.7 %collective-permute-start.13 = (f32[4,3,8,512]{3,2,1,0:T(8,128)S(1)}, f32[4,3,8,512]{3,2,1,0:T(8,128)S(1)}, u32[]{:S(2)}, u32[]{:S(2)}) collective-permute-start(f32[4,3,8,512]{3,2,1,0:T(8,128)S(1)} %pad_maximum_fusion.rest_3_), channel_id=1, source_target_pairs={{0,4},{4,0},{8,12},{12,8},{16,20},{20,16},{24,28},{28,24},{1,5},{5... | collective-permute-start | bytes 589832 | tf_op jit(solution)/shard_map/ppermute | solution.py:572
where the time goes:
time: 84.7 us; the launch traced here: 84.5 us
  starting transfers between devices  31 us (37%)
  Pallas kernels  28.7 us (34%)
  waiting for transfers between devices  22.7 us (27%)
  local copies, waits for them, and re-layouts  1.18 us (1%)
  between operations  0.9 us (1%)
    ppermute x7, waiting for transfers between devices, exchange(): lax.ppermute(blocks[r], axis, [(i, i ^ r) for i in range(count)])  14.5 us
    ppermute x7, starting transfers between devices, exchange(): lax.ppermute(blocks[r], axis, [(i, i ^ r) for i in range(count)])  13.4 us
    pallas_call x1, Pallas kernels, neural(): pl.pallas_call(kernel, out_shape=jax.ShapeDtypeStruct((3, NC, rows), jnp....  11.5 us
    pallas_call x2, Pallas kernels, pair_part(): pl.pallas_call(kernel, out_shape=out_shape, in_specs=[whole_vmem()] * (4...  9.56 us
    all_to_all x1, waiting for transfers between devices, body(): lax.all_to_all(returns, 'bead', split_axis=0, concat_axis=0, tiled=True)  6.57 us
    all_to_all x1, starting transfers between devices, body(): lax.all_to_all(returns, 'bead', split_axis=0, concat_axis=0, tiled=True)  5.99 us
    ppermute x1, starting transfers between devices, body(): upper = lax.ppermute(first, every, back)  4.55 us
    ppermute x3, starting transfers between devices, doubling_step(): got = lax.ppermute(have, axis, [(i, i ^ bit) for i in range(count)])  4.39 us
  transfers between devices with their start and end apart: 15, of which 4 were waited for; matrix products, arithmetic and copies ran while one was open for 0% of the time, Pallas kernels for 28%

commit v1 on v0

--- a/solution.py
+++ b/solution.py
@@ -98,39 +98,41 @@
     rows = atoms // groups
 
     def kernel(place_ref, q_ref, p_ref, f_ref, n_ref, *rest):
-        outs, (p_buf, f_buf, sems) = rest[:groups], rest[groups:]
-        loads = [
-            pltpu.make_async_copy(p_ref, p_buf, sems.at[0]),
-            pltpu.make_async_copy(f_ref, f_buf, sems.at[1]),
-        ]
+        outs, (blocks, kicks, loaded, stored) = rest[:groups], rest[groups:]
+        loads = []
         for r in range(groups):
             at = block_of(place_ref, r, rows)
-            for slot, (ref, first) in enumerate(((q_ref, 0), (n_ref, 6))):
-                loads.append(
-                    pltpu.make_async_copy(
-                        ref.at[:, :, at], outs[r].at[pl.ds(first, 3)], sems.at[2 + 2 * r + slot]
-                    )
-                )
-        for load in loads:
-            load.start()
-        loads[0].wait()
-        loads[1].wait()
+            targets = [blocks.at[r, pl.ds(first, 3)] for first in (0, 3, 6)] + [kicks.at[r]]
+            loads.append(
+                [
+                    pltpu.make_async_copy(ref.at[:, :, at], target, loaded.at[4 * r + i])
+                    for i, (ref, target) in enumerate(zip((q_ref, p_ref, n_ref, f_ref), targets))
+                ]
+            )
+            for load in loads[r]:
+                load.start()
+        stores = []
         for r in range(groups):
-            at = block_of(place_ref, r, rows)
+            for load in loads[r]:
+                load.wait()
             for x in range(3):
-                outs[r][3 + x] = p_buf[x, :, at] + 0.5 * TIME_STEP * f_buf[x, :, at]
-        for load in loads[2:]:
-            load.wait()
-
+                blocks[r, 3 + x] = blocks[r, 3 + x] + 0.5 * TIME_STEP * kicks[r, x]
+            stores.append(pltpu.make_async_copy(blocks.at[r], outs[r], stored.at[r]))
+            stores[r].start()
+        for store in stores:
+            store.wait()
+
+    hbm = pl.BlockSpec(memory_space=pltpu.HBM)
     return pl.pallas_call(
         kernel,
         out_shape=[jax.ShapeDtypeStruct((9, beads, rows), jnp.float32)] * groups,
-        in_specs=[smem()] + [pl.BlockSpec(memory_space=pltpu.HBM)] * 4,
-        out_specs=[whole_vmem()] * groups,
+        in_specs=[smem()] + [hbm] * 4,
+        out_specs=[hbm] * groups,
         scratch_shapes=[
-            pltpu.VMEM((3, beads, atoms), jnp.float32),
-            pltpu.VMEM((3, beads, atoms), jnp.float32),
-            pltpu.SemaphoreType.DMA((2 + 2 * groups,)),
+            pltpu.VMEM((groups, 9, beads, rows), jnp.float32),
+            pltpu.VMEM((groups, 3, beads, rows), jnp.float32),
+            pltpu.SemaphoreType.DMA((4 * groups,)),
+            pltpu.SemaphoreType.DMA((groups,)),
         ],
         compiler_params=params(60),
         name="pack",
@@ -526,45 +528,58 @@
 
 
 def finish(place, pairs, first, fields, neural_parts, partners, coefs):
-    groups, _, beads, size = fields[0].shape
-    rows = size * len(fields)
+    groups, _, beads, rows = fields.shape
     atoms = groups * rows
     counts = [part.shape[0] for part in neural_parts]
 
-    def kernel(place_ref, first_ref, coef_ref, *rest):
+    def kernel(place_ref, first_ref, coef_ref, in_ref, *rest):
         halves, rest = rest[: len(pairs)], rest[len(pairs) :]
-        ins, rest = rest[: len(fields)], rest[len(fields) :]
-        blocks, (newp, newf) = rest[: len(counts)], rest[len(counts) :]
+        blocks, (newp, newf, pair, momenta, forces, sems) = rest[: len(counts)], rest[len(counts) :]
         own = place_ref[0]
         at = 0
         for half in halves:
-            newf[:, :, pl.ds(at, half.shape[2])] = half[...]
+            pair[:, :, pl.ds(at, half.shape[2])] = half[...]
             at += half.shape[2]
-        newf[:, :, pl.ds(0, LANES)] = first_ref[...]
+        pair[:, :, pl.ds(0, LANES)] = first_ref[...]
         coef = [coef_ref[c, own] for c in range(NC)]
         blocks = [block.at[i] for block, count in zip(blocks, counts) for i in range(count)]
-        for r, block in zip(partners, blocks):
+        copies = []
+        for slot, (r, block) in enumerate(zip(partners, blocks)):
             g = own ^ r
             for t in range(0, rows, LANES):
                 at = pl.ds(pl.multiple_of(g * rows + t, LANES), LANES)
-                moved = ins[t // size].at[g, :, :, pl.ds(t % size, LANES)]
+                inner = pl.ds(t, LANES)
                 for x in range(3):
-                    force = newf[x, :, at]
+                    force = pair[x, :, at]
                     for c in range(NC):
-                        force = force + coef[c] * block[x, pl.ds(c, 1), pl.ds(t, LANES)]
-                    newf[x, :, at] = force
-                    newp[x, :, at] = moved[3 + x] + 0.5 * TIME_STEP * force
+                        force = force + coef[c] * block[x, pl.ds(c, 1), inner]
+                    forces[slot, x, :, inner] = force
+                    momenta[slot, x, :, inner] = in_ref[g, 3 + x, :, inner] + 0.5 * TIME_STEP * force
+            at = block_of(place_ref, r, rows)
+            for i, (source, out) in enumerate(((forces, newf), (momenta, newp))):
+                copy = pltpu.make_async_copy(
+                    source.at[slot], out.at[:, :, at], sems.at[2 * slot + i]
+                )
+                copy.start()
+                copies.append(copy)
+        for copy in copies:
+            copy.wait()
 
     out = jax.ShapeDtypeStruct((3, beads, atoms), jnp.float32)
     return pl.pallas_call(
         kernel,
         out_shape=(out,) * 2,
-        in_specs=[smem()]
-        + [whole_vmem()] * (2 + len(pairs) + len(fields) + len(neural_parts)),
-        out_specs=(whole_vmem(),) * 2,
+        in_specs=[smem()] + [whole_vmem()] * (3 + len(pairs) + len(neural_parts)),
+        out_specs=(pl.BlockSpec(memory_space=pltpu.HBM),) * 2,
+        scratch_shapes=[
+            pltpu.VMEM((3, beads, atoms), jnp.float32),
+            pltpu.VMEM((groups, 3, beads, rows), jnp.float32),
+            pltpu.VMEM((groups, 3, beads, rows), jnp.float32),
+            pltpu.SemaphoreType.DMA((2 * groups,)),
+        ],
         compiler_params=params(),
         name="finish",
-    )(place, first, coefs, *pairs, *fields, *neural_parts)
+    )(place, first, coefs, fields, *pairs, *neural_parts)
 
 
 def doubling_step(have, partners, axis, bit):
@@ -649,7 +664,7 @@
     coefs = (kernel * np.float32(BEADS / NC)).reshape(NC, groups, beads, 1)
     coefs = jnp.asarray(np.broadcast_to(coefs, (NC, groups, beads, LANES)))
     new_p, force = finish(
-        place, [*pairs, rest], first, [fields], (have, got), partners, coefs
+        place, [*pairs, rest], first, fields, (have, got), partners, coefs
     )
     return tuple(swap(out) for out in (new_q, new_p, force))
 

time: 84.7 us -> 84.6 us (level)
  no operation moved by 1% of the time
where the time goes in v1:
time: 84.6 us; the launch traced here: 84.3 us
  starting transfers between devices  31 us (37%)
  Pallas kernels  28.4 us (34%)
  waiting for transfers between devices  22.7 us (27%)
  local copies, waits for them, and re-layouts  1.18 us (1%)
  between operations  1.06 us (1%)
    ppermute x7, waiting for transfers between devices, exchange(): lax.ppermute(blocks[r], axis, [(i, i ^ r) for i in range(count)])  14.5 us
    ppermute x7, starting transfers between devices, exchange(): lax.ppermute(blocks[r], axis, [(i, i ^ r) for i in range(count)])  13.4 us
    pallas_call x1, Pallas kernels, neural(): pl.pallas_call(kernel, out_shape=jax.ShapeDtypeStruct((3, NC, rows), jnp....  11.5 us
    pallas_call x2, Pallas kernels, pair_part(): pl.pallas_call(kernel, out_shape=out_shape, in_specs=[whole_vmem()] * (4...  9.56 us
    all_to_all x1, waiting for transfers between devices, body(): lax.all_to_all(returns, 'bead', split_axis=0, concat_axis=0, tiled=True)  6.57 us
    all_to_all x1, starting transfers between devices, body(): lax.all_to_all(returns, 'bead', split_axis=0, concat_axis=0, tiled=True)  5.99 us
    ppermute x1, starting transfers between devices, body(): upper = lax.ppermute(first, every, back)  4.55 us
    ppermute x3, starting transfers between devices, doubling_step(): got = lax.ppermute(have, axis, [(i, i ^ bit) for i in range(count)])  4.4 us
  transfers between devices with their start and end apart: 15, of which 4 were waited for; matrix products, arithmetic and copies ran while one was open for 0% of the time, Pallas kernels for 28%

profile of v1, /device:TPU:0, one launch (start us, length us, event | category | flops | bytes accessed | tf_op | source)
XLA Modules:
  0.0 84.3 jit_solution(1582641179385349645)
XLA Ops:
  0.6 0.0 copy-start.10
  0.7 2.5 %pack.1 = (f32[9,8,512]{2,1,0:T(8,128)}, f32[9,8,512]{2,1,0:T(8,128)}, f32[9,8,512]{2,1,0:T(8,128)}, f32[9,8,512]{2,1,0:T(8,128)}, f32[9,8,512]{2,1,0:T(8,128)},...) custom-call(s32[1]{0:T(128)} %bitcast.place_ref, f32[3,8,4096]{2,1,0:T(8,128)} %bitcast.26, ...), custom_call_target="tpu_custom_call" | custom-call | tf_op jit(solution)/shard_map/pack/pallas_call | solution.py:126
  3.2 3.0 %collective-permute-start = (f32[9,8,512]{2,1,0:T(8,128)}, f32[9,8,512]{2,1,0:T(8,128)S(1)}, u32[]{:S(2)}, u32[]{:S(2)}) collective-permute-start(f32[9,8,512]{2,1,0:T(8,128)} %get-tuple-element.52), channel_id=1, source_target_pairs={{0,4},{4,0},{8,12},{12,8},{16,20},{20,16},{24,28},{28,24},{1,5},{5... | collective-permute-start | bytes 442376 | tf_op jit(solution)/shard_map/ppermute | solution.py:92
  6.2 1.6 %collective-permute-start.1 = (f32[9,8,512]{2,1,0:T(8,128)}, f32[9,8,512]{2,1,0:T(8,128)S(1)}, u32[]{:S(2)}, u32[]{:S(2)}) collective-permute-start(f32[9,8,512]{2,1,0:T(8,128)} %get-tuple-element.53), channel_id=1, source_target_pairs={{0,8},{4,12},{8,0},{12,4},{16,24},{20,28},{24,16},{28,20},{1,9},{5... | collective-permute-start | bytes 442376 | tf_op jit(solution)/shard_map/ppermute | solution.py:92
  7.8 0.0 collective-permute-start.2
  7.8 3.0 %collective-permute-start.3 = (f32[9,8,512]{2,1,0:T(8,128)}, f32[9,8,512]{2,1,0:T(8,128)S(1)}, u32[]{:S(2)}, u32[]{:S(2)}) collective-permute-start(f32[9,8,512]{2,1,0:T(8,128)} %get-tuple-element.55), channel_id=1, source_target_pairs={{0,16},{4,20},{8,24},{12,28},{16,0},{20,4},{24,8},{28,12},{1,17},{... | collective-permute-start | bytes 442376 | tf_op jit(solution)/shard_map/ppermute | solution.py:92
  10.8 1.3 %collective-permute-start.4 = (f32[9,8,512]{2,1,0:T(8,128)}, f32[9,8,512]{2,1,0:T(8,128)S(1)}, u32[]{:S(2)}, u32[]{:S(2)}) collective-permute-start(f32[9,8,512]{2,1,0:T(8,128)} %get-tuple-element.56), channel_id=1, source_target_pairs={{0,20},{4,16},{8,28},{12,24},{16,4},{20,0},{24,12},{28,8},{1,21},{... | collective-permute-start | bytes 442376 | tf_op jit(solution)/shard_map/ppermute | solution.py:92
  12.0 0.0 collective-permute-done.rest_0_
  12.0 3.6 %collective-permute-start.5 = (f32[9,8,512]{2,1,0:T(8,128)}, f32[9,8,512]{2,1,0:T(8,128)S(1)}, u32[]{:S(2)}, u32[]{:S(2)}) collective-permute-start(f32[9,8,512]{2,1,0:T(8,128)} %get-tuple-element.57), channel_id=1, source_target_pairs={{0,24},{4,28},{8,16},{12,20},{16,8},{20,12},{24,0},{28,4},{1,25},{... | collective-permute-start | bytes 442376 | tf_op jit(solution)/shard_map/ppermute | solution.py:92
  15.6 2.7 %collective-permute-done.1.rest_1_ = f32[9,8,512]{2,1,0:T(8,128)S(1)} collective-permute-done((f32[9,8,512]{2,1,0:T(8,128)}, f32[9,8,512]{2,1,0:T(8,128)S(1)}, u32[]{:S(2)}, u32[]{:S(2)}) %collective-permute-start.1) | collective-permute-done | bytes 147488 | tf_op jit(solution)/shard_map/ppermute | solution.py:92
  18.4 0.9 %collective-permute-start.6 = (f32[9,8,512]{2,1,0:T(8,128)}, f32[9,8,512]{2,1,0:T(8,128)S(1)}, u32[]{:S(2)}, u32[]{:S(2)}) collective-permute-start(f32[9,8,512]{2,1,0:T(8,128)} %get-tuple-element.58), channel_id=1, source_target_pairs={{0,28},{4,24},{8,20},{12,16},{16,12},{20,8},{24,4},{28,0},{1,29},{... | collective-permute-start | bytes 442376 | tf_op jit(solution)/shard_map/ppermute | solution.py:92
  19.3 0.0 copy-start.4
  19.3 1.0 %copy-done.4 = bf16[128,1600]{0,1:T(8,128)(2,1)S(1)} copy-done((bf16[128,1600]{0,1:T(8,128)(2,1)S(1)}, bf16[128,1600]{0,1:T(8,128)(2,1)}, u32[]{:S(2)}) %copy-start.4) | copy-done | bytes 409624
  20.3 0.4 prepare.1
  20.7 0.0 copy-start.9
  20.7 0.0 collective-permute-done.2.rest_2_
  20.7 0.0 collective-permute-done.3.rest_3_
  20.7 11.7 %collective-permute-done.4.rest_4_ = f32[9,8,512]{2,1,0:T(8,128)S(1)} collective-permute-done((f32[9,8,512]{2,1,0:T(8,128)}, f32[9,8,512]{2,1,0:T(8,128)S(1)}, u32[]{:S(2)}, u32[]{:S(2)}) %collective-permute-start.4) | collective-permute-done | bytes 147488 | tf_op jit(solution)/shard_map/ppermute | solution.py:92
  32.4 0.0 collective-permute-done.5.rest_5_
  32.4 0.0 collective-permute-done.6.rest_6_
  32.5 0.9 %contract.1 = (f32[3,8,512]{2,1,0:T(8,128)S(1)}, f32[3,8,128]{2,1,0:T(8,128)S(1)}, f32[3,8,128]{2,1,0:T(8,128)S(1)}, f32[3,3,8,8,512]{4,3,2,1,0:T(8,128)S(1)}) custom-call(s32[1]{0:T(128)} %bitcast.place_ref, f32[1,512]{1,0:T(1,128)S(1)} %get-tuple-element.64.mass_ref, f32[8,192]{1,0:T(8,128)S(1)} %copy-done.1, f32[9,8,512]{2,1,0:T(8,128)S(1)} %copy-done, ...), custom_call_target="tpu_custom_call" | custom-call | tf_op jit(solution)/shard_map/contract/pallas_call | solution.py:219
  33.4 0.8 %collective-permute-start.7 = (f32[3,8,128]{2,1,0:T(8,128)S(1)}, f32[3,8,128]{2,1,0:T(8,128)S(1)}, u32[]{:S(2)}, u32[]{:S(2)}) collective-permute-start(f32[3,8,128]{2,1,0:T(8,128)S(1)} %get-tuple-element.74), channel_id=1, source_target_pairs={{0,4},{1,5},{2,6},{3,7},{4,8},{5,9},{6,10},{7,11},{8,12},{9,13},{1... | collective-permute-start | bytes 36872 | tf_op jit(solution)/shard_map/ppermute | solution.py:631
  34.3 4.6 %collective-permute-start.8 = (f32[3,8,128]{2,1,0:T(8,128)S(1)}, f32[3,8,128]{2,1,0:T(8,128)S(1)}, u32[]{:S(2)}, u32[]{:S(2)}) collective-permute-start(f32[3,8,128]{2,1,0:T(8,128)S(1)} %get-tuple-element.75), channel_id=1, source_target_pairs={{4,0},{5,1},{6,2},{7,3},{8,4},{9,5},{10,6},{11,7},{12,8},{13,9},{1... | collective-permute-start | bytes 36872 | tf_op jit(solution)/shard_map/ppermute | solution.py:632
  38.8 1.6 %transform.1 = f32[8,6,8,512]{3,2,1,0:T(8,128)} custom-call(f32[3,3,8,8,512]{4,3,2,1,0:T(8,128)S(1)} %get-tuple-element.73.fields_ref, f32[1,512]{1,0:T(1,128)S(1)} %get-tuple-element.64.mass_ref, f32[128,192]{1,0:T(8,128)S(1)} %copy-done.9), custom_call_target="tpu_custom_call" | custom-call | flops 1000000000 | bytes 2000000 | tf_op jit(solution)/shard_map/transform/pallas_call | solution.py:260
  40.5 0.0 copy-start.5
  40.5 0.0 copy-start.6
  40.5 0.0 copy-start.8
  40.5 0.0 collective-permute-done.7.low_ref
  40.5 1.7 %collective-permute-done.8.up_ref = f32[3,8,128]{2,1,0:T(8,128)S(1)} collective-permute-done((f32[3,8,128]{2,1,0:T(8,128)S(1)}, f32[3,8,128]{2,1,0:T(8,128)S(1)}, u32[]{:S(2)}, u32[]{:S(2)}) %collective-permute-start.8) | collective-permute-done | bytes 12320 | tf_op jit(solution)/shard_map/ppermute | solution.py:632
  42.2 6.0 %all-to-all-start = ((f32[8,6,8,512]{3,2,1,0:T(8,128)}), f32[8,6,8,512]{3,2,1,0:T(8,128)S(1)}, u32[]{:S(2)}, u32[]{:S(2)}) async-start(f32[8,6,8,512]{3,2,1,0:T(8,128)} %transform.1), calls=%async_computation | async-start | bytes 1572864 | tf_op jit(solution)/shard_map/all_to_all | solution.py:635
  48.2 11.5 %neural.1 = f32[3,8,512]{2,1,0:T(8,128)S(1)} custom-call(f32[3,8,512]{2,1,0:T(8,128)S(1)} %get-tuple-element.77.c_ref, f32[3,8,128]{2,1,0:T(8,128)S(1)} %collective-permute-done.7.low_ref, f32[3,8,128]{2,1,0:T(8,128)S(1)} %collective-permute-done.8.up_ref, s32[32,512]{1,0:T(8,128)S(1)} %get-tuple-element.80.list_ref, ...), custom_call_target="tpu_custom_call" | custom-call | flops 12000000000 | bytes 4000000 | tf_op jit(solution)/shard_map/neural/pallas_call | solution.py:384
  59.7 2.9 %collective-permute-start.9 = (f32[1,3,8,512]{3,2,1,0:T(8,128)S(1)}, f32[1,3,8,512]{3,2,1,0:T(8,128)S(1)}, u32[]{:S(2)}, u32[]{:S(2)}) collective-permute-start(f32[1,3,8,512]{3,2,1,0:T(8,128)S(1)} %bitcast.18), channel_id=1, source_target_pairs={{0,16},{4,20},{8,24},{12,28},{16,0},{20,4},{24,8},{28,12},{1,17},{... | collective-permute-start | bytes 147464 | tf_op jit(solution)/shard_map/ppermute | solution.py:587
  62.7 6.6 %all-to-all-done.in_ref = f32[8,6,8,512]{3,2,1,0:T(8,128)S(1)} async-done(((f32[8,6,8,512]{3,2,1,0:T(8,128)}), f32[8,6,8,512]{3,2,1,0:T(8,128)S(1)}, u32[]{:S(2)}, u32[]{:S(2)}) %all-to-all-start) | async-done | bytes 786464 | tf_op jit(solution)/shard_map/all_to_all | solution.py:635
  69.2 0.8 assemble.1
  70.0 0.0 collective-permute-done.9
  70.0 0.1 collective-permute-start.10
  70.1 0.1 collective-permute-start.11
  70.2 1.7 %collective-permute-start.12 = (f32[3,8,128]{2,1,0:T(8,128)S(1)}, f32[3,8,128]{2,1,0:T(8,128)S(1)}, u32[]{:S(2)}, u32[]{:S(2)}) collective-permute-start(f32[3,8,128]{2,1,0:T(8,128)S(1)} %get-tuple-element.99), channel_id=1, source_target_pairs={{1,0},{2,1},{3,2},{0,3},{5,4},{6,5},{7,6},{4,7},{9,8},{10,9},{11,1... | collective-permute-start | bytes 36872 | tf_op jit(solution)/shard_map/ppermute | solution.py:647
  71.9 3.2 %pair_0.1.rest_0_ = f32[3,8,1536]{2,1,0:T(8,128)S(1)} custom-call(s32[3,4,4096]{2,1,0:T(4,128)S(1)} %get-tuple-element.91.words_ref, f32[3,8,4096]{2,1,0:T(8,128)S(1)} %get-tuple-element.87.fixed_ref, f32[8,128]{1,0:T(8,128)S(1)} %get-tuple-element.88.unit_ref, s32[32,4096]{1,0:T(8,128)S(1)} %get-tuple-element.89.list_ref), custom_call_target="tpu_custom_call" | custom-call | flops 3600000000 | bytes 2000000 | tf_op jit(solution)/shard_map/pair_0/pallas_call | solution.py:516
  75.2 0.0 collective-permute-done.10
  75.2 0.0 copy-start.11
  75.2 1.4 %collective-permute-start.13 = (f32[4,3,8,512]{3,2,1,0:T(8,128)S(1)}, f32[4,3,8,512]{3,2,1,0:T(8,128)S(1)}, u32[]{:S(2)}, u32[]{:S(2)}) collective-permute-start(f32[4,3,8,512]{3,2,1,0:T(8,128)S(1)} %pad_maximum_fusion.rest_2_), channel_id=1, source_target_pairs={{0,4},{4,0},{8,12},{12,8},{16,20},{20,16},{24,28},{28,24},{1,5},{5... | collective-permute-start | bytes 589832 | tf_op jit(solution)/shard_map/ppermute | solution.py:587
  76.6 0.0 collective-permute-done.11.rest_1_
  76.6 0.0 collective-permute-done.12.rest_2_
  76.6 6.3 %pair_12.1 = (f32[3,8,2560]{2,1,0:T(8,128)S(1)}, f32[3,8,128]{2,1,0:T(8,128)S(1)}) custom-call(s32[3,4,4096]{2,1,0:T(4,128)S(1)} %get-tuple-element.91.words_ref, f32[3,8,4096]{2,1,0:T(8,128)S(1)} %get-tuple-element.87.fixed_ref, f32[8,128]{1,0:T(8,128)S(1)} %get-tuple-element.88.unit_ref, s32[32,4096]{1,0:T(8,128)S(1)} %get-tuple-element.89.list_ref, ...), custom_call_target="tpu_custom_call" | custom-call | flops 6000000000 | bytes 2000000 | tf_op jit(solution)/shard_map/pair_12/pallas_call | solution.py:516
  82.9 0.0 collective-permute-done.13.rest_3_
  83.0 0.1 jit_solution_.3.coef_ref
  83.1 1.1 %finish.1 = (f32[3,8,4096]{2,1,0:T(8,128)}, f32[3,8,4096]{2,1,0:T(8,128)}) custom-call(s32[1]{0:T(128)} %bitcast.place_ref, f32[3,8,128]{2,1,0:T(8,128)S(1)} %get-tuple-element.93.first_ref, f32[8,8,8,128]{3,2,1,0:T(8,128)S(1)} %jit_solution_.3.coef_ref, f32[8,6,8,512]{3,2,1,0:T(8,128)S(1)} %all-to-all-done.in_ref, f32[3,8,1536]{2,1,0:T(8,128)S(1)} %pair_0.1.rest_0_, ...), custom_call_target="tpu_custom_call" | custom-call | tf_op jit(solution)/shard_map/finish/pallas_call | solution.py:569
  (19 shorter events, 0.1 us)
Async XLA Ops:
  0.6 18.7 %copy-start.10 = (bf16[128,128]{1,0:T(8,128)(2,1)S(1)}, bf16[128,128]{1,0:T(8,128)(2,1)}, u32[]{:S(2)}) copy-start(bf16[128,128]{1,0:T(8,128)(2,1)} %constant.14.clone.order_ref) | copy-start | bytes 98308
  0.6 18.7 %copy-start.3 = (s32[4096,32]{0,1:T(8,128)S(1)}, s32[4096,32]{0,1:T(8,128)}, u32[]{:S(2)}) copy-start(s32[4096,32]{0,1:T(8,128)} %param.20) | copy-start | bytes 1572868
  0.7 18.7 %copy-start.7 = (f32[4096]{0:T(1024)S(1)}, f32[4096]{0:T(1024)}, u32[]{:S(2)}) copy-start(f32[4096]{0:T(1024)} %param.19) | copy-start | bytes 49156
  0.7 18.7 %copy-start.2 = (bf16[1600,240]{0,1:T(8,128)(2,1)S(1)}, bf16[1600,240]{0,1:T(8,128)(2,1)}, u32[]{:S(2)}) copy-start(bf16[1600,240]{0,1:T(8,128)(2,1)} %param.22) | copy-start | bytes 2304004
  3.2 8.9 %collective-permute-start = (f32[9,8,512]{2,1,0:T(8,128)}, f32[9,8,512]{2,1,0:T(8,128)S(1)}, u32[]{:S(2)}, u32[]{:S(2)}) collective-permute-start(f32[9,8,512]{2,1,0:T(8,128)} %get-tuple-element.52), channel_id=1, source_target_pairs={{0,4},{4,0},{8,12},{12,8},{16,20},{20,16},{24,28},{28,24},{1,5},{5... | collective-permute-start | bytes 442376 | tf_op jit(solution)/shard_map/ppermute | solution.py:92
  6.2 12.2 %collective-permute-start.1 = (f32[9,8,512]{2,1,0:T(8,128)}, f32[9,8,512]{2,1,0:T(8,128)S(1)}, u32[]{:S(2)}, u32[]{:S(2)}) collective-permute-start(f32[9,8,512]{2,1,0:T(8,128)} %get-tuple-element.53), channel_id=1, source_target_pairs={{0,8},{4,12},{8,0},{12,4},{16,24},{20,28},{24,16},{28,20},{1,9},{5... | collective-permute-start | bytes 442376 | tf_op jit(solution)/shard_map/ppermute | solution.py:92
  7.8 12.9 %collective-permute-start.2 = (f32[9,8,512]{2,1,0:T(8,128)}, f32[9,8,512]{2,1,0:T(8,128)S(1)}, u32[]{:S(2)}, u32[]{:S(2)}) collective-permute-start(f32[9,8,512]{2,1,0:T(8,128)} %get-tuple-element.54), channel_id=1, source_target_pairs={{0,12},{4,8},{8,4},{12,0},{16,28},{20,24},{24,20},{28,16},{1,13},{... | collective-permute-start | bytes 442376 | tf_op jit(solution)/shard_map/ppermute | solution.py:92
  7.8 13.0 %collective-permute-start.3 = (f32[9,8,512]{2,1,0:T(8,128)}, f32[9,8,512]{2,1,0:T(8,128)S(1)}, u32[]{:S(2)}, u32[]{:S(2)}) collective-permute-start(f32[9,8,512]{2,1,0:T(8,128)} %get-tuple-element.55), channel_id=1, source_target_pairs={{0,16},{4,20},{8,24},{12,28},{16,0},{20,4},{24,8},{28,12},{1,17},{... | collective-permute-start | bytes 442376 | tf_op jit(solution)/shard_map/ppermute | solution.py:92
  10.8 21.7 %collective-permute-start.4 = (f32[9,8,512]{2,1,0:T(8,128)}, f32[9,8,512]{2,1,0:T(8,128)S(1)}, u32[]{:S(2)}, u32[]{:S(2)}) collective-permute-start(f32[9,8,512]{2,1,0:T(8,128)} %get-tuple-element.56), channel_id=1, source_target_pairs={{0,20},{4,16},{8,28},{12,24},{16,4},{20,0},{24,12},{28,8},{1,21},{... | collective-permute-start | bytes 442376 | tf_op jit(solution)/shard_map/ppermute | solution.py:92
  12.0 20.4 %collective-permute-start.5 = (f32[9,8,512]{2,1,0:T(8,128)}, f32[9,8,512]{2,1,0:T(8,128)S(1)}, u32[]{:S(2)}, u32[]{:S(2)}) collective-permute-start(f32[9,8,512]{2,1,0:T(8,128)} %get-tuple-element.57), channel_id=1, source_target_pairs={{0,24},{4,28},{8,16},{12,20},{16,8},{20,12},{24,0},{28,4},{1,25},{... | collective-permute-start | bytes 442376 | tf_op jit(solution)/shard_map/ppermute | solution.py:92
  18.4 14.1 %collective-permute-start.6 = (f32[9,8,512]{2,1,0:T(8,128)}, f32[9,8,512]{2,1,0:T(8,128)S(1)}, u32[]{:S(2)}, u32[]{:S(2)}) collective-permute-start(f32[9,8,512]{2,1,0:T(8,128)} %get-tuple-element.58), channel_id=1, source_target_pairs={{0,28},{4,24},{8,20},{12,16},{16,12},{20,8},{24,4},{28,0},{1,29},{... | collective-permute-start | bytes 442376 | tf_op jit(solution)/shard_map/ppermute | solution.py:92
  19.3 1.0 %copy-start.4 = (bf16[128,1600]{0,1:T(8,128)(2,1)S(1)}, bf16[128,1600]{0,1:T(8,128)(2,1)}, u32[]{:S(2)}) copy-start(bf16[128,1600]{0,1:T(8,128)(2,1)} %param.21) | copy-start | bytes 1228804
  20.3 12.1 %copy-start = (f32[9,8,512]{2,1,0:T(8,128)S(1)}, f32[9,8,512]{2,1,0:T(8,128)}, u32[]{:S(2)}) copy-start(f32[9,8,512]{2,1,0:T(8,128)} %get-tuple-element.65.own_ref) | copy-start | bytes 442372
  20.3 12.1 %copy-start.1 = (f32[8,192]{1,0:T(8,128)S(1)}, f32[8,192]{1,0:T(8,128)}, u32[]{:S(2)}) copy-start(f32[8,192]{1,0:T(8,128)} %constant.15.clone.table_ref) | copy-start | bytes 18436
  20.7 18.1 %copy-start.9 = (f32[128,192]{1,0:T(8,128)S(1)}, f32[128,192]{1,0:T(8,128)}, u32[]{:S(2)}) copy-start(f32[128,192]{1,0:T(8,128)} %constant.16.clone.table_ref) | copy-start | bytes 294916
  33.4 7.1 %collective-permute-start.7 = (f32[3,8,128]{2,1,0:T(8,128)S(1)}, f32[3,8,128]{2,1,0:T(8,128)S(1)}, u32[]{:S(2)}, u32[]{:S(2)}) collective-permute-start(f32[3,8,128]{2,1,0:T(8,128)S(1)} %get-tuple-element.74), channel_id=1, source_target_pairs={{0,4},{1,5},{2,6},{3,7},{4,8},{5,9},{6,10},{7,11},{8,12},{9,13},{1... | collective-permute-start | bytes 36872 | tf_op jit(solution)/shard_map/ppermute | solution.py:631
  34.3 7.9 %collective-permute-start.8 = (f32[3,8,128]{2,1,0:T(8,128)S(1)}, f32[3,8,128]{2,1,0:T(8,128)S(1)}, u32[]{:S(2)}, u32[]{:S(2)}) collective-permute-start(f32[3,8,128]{2,1,0:T(8,128)S(1)} %get-tuple-element.75), channel_id=1, source_target_pairs={{4,0},{5,1},{6,2},{7,3},{8,4},{9,5},{10,6},{11,7},{12,8},{13,9},{1... | collective-permute-start | bytes 36872 | tf_op jit(solution)/shard_map/ppermute | solution.py:632
  40.5 7.7 %copy-start.5 = (bf16[240,240]{1,0:T(8,128)(2,1)S(1)}, bf16[240,240]{1,0:T(8,128)(2,1)}, u32[]{:S(2)}) copy-start(bf16[240,240]{1,0:T(8,128)(2,1)} %w2.1) | copy-start | bytes 345604
  40.5 7.7 %copy-start.6 = (bf16[240,240]{1,0:T(8,128)(2,1)S(1)}, bf16[240,240]{1,0:T(8,128)(2,1)}, u32[]{:S(2)}) copy-start(bf16[240,240]{1,0:T(8,128)(2,1)} %w3.1) | copy-start | bytes 345604
  40.5 7.7 %copy-start.8 = (bf16[240,3]{0,1:T(4,128)(2,1)S(1)}, bf16[240,3]{0,1:T(4,128)(2,1)}, u32[]{:S(2)}) copy-start(bf16[240,3]{0,1:T(4,128)(2,1)} %param.25) | copy-start | bytes 4324
  42.2 27.1 %all-to-all-start = ((f32[8,6,8,512]{3,2,1,0:T(8,128)}), f32[8,6,8,512]{3,2,1,0:T(8,128)S(1)}, u32[]{:S(2)}, u32[]{:S(2)}) async-start(f32[8,6,8,512]{3,2,1,0:T(8,128)} %transform.1), calls=%async_computation | async-start | bytes 1572864 | tf_op jit(solution)/shard_map/all_to_all | solution.py:635
  59.7 10.3 %collective-permute-start.9 = (f32[1,3,8,512]{3,2,1,0:T(8,128)S(1)}, f32[1,3,8,512]{3,2,1,0:T(8,128)S(1)}, u32[]{:S(2)}, u32[]{:S(2)}) collective-permute-start(f32[1,3,8,512]{3,2,1,0:T(8,128)S(1)} %bitcast.18), channel_id=1, source_target_pairs={{0,16},{4,20},{8,24},{12,28},{16,0},{20,4},{24,8},{28,12},{1,17},{... | collective-permute-start | bytes 147464 | tf_op jit(solution)/shard_map/ppermute | solution.py:587
  70.0 5.1 %collective-permute-start.10 = (f32[2,3,8,512]{3,2,1,0:T(8,128)S(1)}, f32[2,3,8,512]{3,2,1,0:T(8,128)S(1)}, u32[]{:S(2)}, u32[]{:S(2)}) collective-permute-start(f32[2,3,8,512]{3,2,1,0:T(8,128)S(1)} %pad_maximum_fusion.1), channel_id=1, source_target_pairs={{0,8},{4,12},{8,0},{12,4},{16,24},{20,28},{24,16},{28,20},{1,9},{5... | collective-permute-start | bytes 294920 | tf_op jit(solution)/shard_map/ppermute | solution.py:587
  70.1 6.5 %collective-permute-start.11 = (f32[3,8,128]{2,1,0:T(8,128)S(1)}, f32[3,8,128]{2,1,0:T(8,128)S(1)}, u32[]{:S(2)}, u32[]{:S(2)}) collective-permute-start(f32[3,8,128]{2,1,0:T(8,128)S(1)} %get-tuple-element.100), channel_id=1, source_target_pairs={{0,1},{1,2},{2,3},{3,0},{4,5},{5,6},{6,7},{7,4},{8,9},{9,10},{10,1... | collective-permute-start | bytes 36872 | tf_op jit(solution)/shard_map/ppermute | solution.py:646
  70.2 6.4 %collective-permute-start.12 = (f32[3,8,128]{2,1,0:T(8,128)S(1)}, f32[3,8,128]{2,1,0:T(8,128)S(1)}, u32[]{:S(2)}, u32[]{:S(2)}) collective-permute-start(f32[3,8,128]{2,1,0:T(8,128)S(1)} %get-tuple-element.99), channel_id=1, source_target_pairs={{1,0},{2,1},{3,2},{0,3},{5,4},{6,5},{7,6},{4,7},{9,8},{10,9},{11,1... | collective-permute-start | bytes 36872 | tf_op jit(solution)/shard_map/ppermute | solution.py:647
  75.2 7.8 %copy-start.11 = (f32[8,8,8]{2,1,0:T(8,128)S(1)}, f32[8,8,8]{2,1,0:T(8,128)}, u32[]{:S(2)}) copy-start(f32[8,8,8]{2,1,0:T(8,128)} %constant.17.clone) | copy-start | bytes 6148
  75.2 7.7 %collective-permute-start.13 = (f32[4,3,8,512]{3,2,1,0:T(8,128)S(1)}, f32[4,3,8,512]{3,2,1,0:T(8,128)S(1)}, u32[]{:S(2)}, u32[]{:S(2)}) collective-permute-start(f32[4,3,8,512]{3,2,1,0:T(8,128)S(1)} %pad_maximum_fusion.rest_2_), channel_id=1, source_target_pairs={{0,4},{4,0},{8,12},{12,8},{16,20},{20,16},{24,28},{28,24},{1,5},{5... | collective-permute-start | bytes 589832 | tf_op jit(solution)/shard_map/ppermute | solution.py:587

commit v2 on v1

--- a/solution.py
+++ b/solution.py
@@ -323,7 +323,7 @@
     for f in range(0, desc, chunk):
         size = min(chunk, desc - f)
         first = jnp.dot(inputs, w0_ref[:, pl.ds(f, size)], preferred_element_type=jnp.float32)
-        first = jnp.tanh(first.astype(jnp.bfloat16))
+        first = jnp.tanh(first).astype(jnp.bfloat16)
         part = jnp.dot(first, w1_ref[pl.ds(f, size), :], preferred_element_type=jnp.float32)
         total = part if total is None else total + part
         for _ in range(6):

time: 84.6 us -> 84.6 us (level)
  no operation moved by 1% of the time
where the time goes in v2:
time: 84.6 us; the launch traced here: 84.3 us
  starting transfers between devices  31 us (37%)
  Pallas kernels  28.4 us (34%)
  waiting for transfers between devices  22.7 us (27%)
  local copies, waits for them, and re-layouts  1.18 us (1%)
  between operations  1.06 us (1%)
    ppermute x7, waiting for transfers between devices, exchange(): lax.ppermute(blocks[r], axis, [(i, i ^ r) for i in range(count)])  14.5 us
    ppermute x7, starting transfers between devices, exchange(): lax.ppermute(blocks[r], axis, [(i, i ^ r) for i in range(count)])  13.4 us
    pallas_call x1, Pallas kernels, neural(): pl.pallas_call(kernel, out_shape=jax.ShapeDtypeStruct((3, NC, rows), jnp....  11.6 us
    pallas_call x2, Pallas kernels, pair_part(): pl.pallas_call(kernel, out_shape=out_shape, in_specs=[whole_vmem()] * (4...  9.56 us
    all_to_all x1, waiting for transfers between devices, body(): lax.all_to_all(returns, 'bead', split_axis=0, concat_axis=0, tiled=True)  6.56 us
    all_to_all x1, starting transfers between devices, body(): lax.all_to_all(returns, 'bead', split_axis=0, concat_axis=0, tiled=True)  5.99 us
    ppermute x1, starting transfers between devices, body(): upper = lax.ppermute(first, every, back)  4.55 us
    ppermute x3, starting transfers between devices, doubling_step(): got = lax.ppermute(have, axis, [(i, i ^ bit) for i in range(count)])  4.4 us
  transfers between devices with their start and end apart: 15, of which 4 were waited for; matrix products, arithmetic and copies ran while one was open for 0% of the time, Pallas kernels for 28%

profile of v2, /device:TPU:0, one launch (start us, length us, event | category | flops | bytes accessed | tf_op | source)
XLA Modules:
  0.0 84.3 jit_solution(17482688594965779999)
XLA Ops:
  0.6 0.0 copy-start.10
  0.7 2.5 %pack.1 = (f32[9,8,512]{2,1,0:T(8,128)}, f32[9,8,512]{2,1,0:T(8,128)}, f32[9,8,512]{2,1,0:T(8,128)}, f32[9,8,512]{2,1,0:T(8,128)}, f32[9,8,512]{2,1,0:T(8,128)},...) custom-call(s32[1]{0:T(128)} %bitcast.place_ref, f32[3,8,4096]{2,1,0:T(8,128)} %bitcast.26, ...), custom_call_target="tpu_custom_call" | custom-call | tf_op jit(solution)/shard_map/pack/pallas_call | solution.py:126
  3.2 3.0 %collective-permute-start = (f32[9,8,512]{2,1,0:T(8,128)}, f32[9,8,512]{2,1,0:T(8,128)S(1)}, u32[]{:S(2)}, u32[]{:S(2)}) collective-permute-start(f32[9,8,512]{2,1,0:T(8,128)} %get-tuple-element.52), channel_id=1, source_target_pairs={{0,4},{4,0},{8,12},{12,8},{16,20},{20,16},{24,28},{28,24},{1,5},{5... | collective-permute-start | bytes 442376 | tf_op jit(solution)/shard_map/ppermute | solution.py:92
  6.2 1.6 %collective-permute-start.1 = (f32[9,8,512]{2,1,0:T(8,128)}, f32[9,8,512]{2,1,0:T(8,128)S(1)}, u32[]{:S(2)}, u32[]{:S(2)}) collective-permute-start(f32[9,8,512]{2,1,0:T(8,128)} %get-tuple-element.53), channel_id=1, source_target_pairs={{0,8},{4,12},{8,0},{12,4},{16,24},{20,28},{24,16},{28,20},{1,9},{5... | collective-permute-start | bytes 442376 | tf_op jit(solution)/shard_map/ppermute | solution.py:92
  7.8 0.0 collective-permute-start.2
  7.8 3.0 %collective-permute-start.3 = (f32[9,8,512]{2,1,0:T(8,128)}, f32[9,8,512]{2,1,0:T(8,128)S(1)}, u32[]{:S(2)}, u32[]{:S(2)}) collective-permute-start(f32[9,8,512]{2,1,0:T(8,128)} %get-tuple-element.55), channel_id=1, source_target_pairs={{0,16},{4,20},{8,24},{12,28},{16,0},{20,4},{24,8},{28,12},{1,17},{... | collective-permute-start | bytes 442376 | tf_op jit(solution)/shard_map/ppermute | solution.py:92
  10.8 1.3 %collective-permute-start.4 = (f32[9,8,512]{2,1,0:T(8,128)}, f32[9,8,512]{2,1,0:T(8,128)S(1)}, u32[]{:S(2)}, u32[]{:S(2)}) collective-permute-start(f32[9,8,512]{2,1,0:T(8,128)} %get-tuple-element.56), channel_id=1, source_target_pairs={{0,20},{4,16},{8,28},{12,24},{16,4},{20,0},{24,12},{28,8},{1,21},{... | collective-permute-start | bytes 442376 | tf_op jit(solution)/shard_map/ppermute | solution.py:92
  12.0 0.0 collective-permute-done.rest_0_
  12.0 3.6 %collective-permute-start.5 = (f32[9,8,512]{2,1,0:T(8,128)}, f32[9,8,512]{2,1,0:T(8,128)S(1)}, u32[]{:S(2)}, u32[]{:S(2)}) collective-permute-start(f32[9,8,512]{2,1,0:T(8,128)} %get-tuple-element.57), channel_id=1, source_target_pairs={{0,24},{4,28},{8,16},{12,20},{16,8},{20,12},{24,0},{28,4},{1,25},{... | collective-permute-start | bytes 442376 | tf_op jit(solution)/shard_map/ppermute | solution.py:92
  15.6 2.7 %collective-permute-done.1.rest_1_ = f32[9,8,512]{2,1,0:T(8,128)S(1)} collective-permute-done((f32[9,8,512]{2,1,0:T(8,128)}, f32[9,8,512]{2,1,0:T(8,128)S(1)}, u32[]{:S(2)}, u32[]{:S(2)}) %collective-permute-start.1) | collective-permute-done | bytes 147488 | tf_op jit(solution)/shard_map/ppermute | solution.py:92
  18.4 0.9 %collective-permute-start.6 = (f32[9,8,512]{2,1,0:T(8,128)}, f32[9,8,512]{2,1,0:T(8,128)S(1)}, u32[]{:S(2)}, u32[]{:S(2)}) collective-permute-start(f32[9,8,512]{2,1,0:T(8,128)} %get-tuple-element.58), channel_id=1, source_target_pairs={{0,28},{4,24},{8,20},{12,16},{16,12},{20,8},{24,4},{28,0},{1,29},{... | collective-permute-start | bytes 442376 | tf_op jit(solution)/shard_map/ppermute | solution.py:92
  19.3 0.0 copy-start.4
  19.3 1.0 %copy-done.4 = bf16[128,1600]{0,1:T(8,128)(2,1)S(1)} copy-done((bf16[128,1600]{0,1:T(8,128)(2,1)S(1)}, bf16[128,1600]{0,1:T(8,128)(2,1)}, u32[]{:S(2)}) %copy-start.4) | copy-done | bytes 409624
  20.3 0.4 prepare.1
  20.7 0.0 copy-start.9
  20.7 0.0 collective-permute-done.2.rest_2_
  20.7 0.0 collective-permute-done.3.rest_3_
  20.7 11.7 %collective-permute-done.4.rest_4_ = f32[9,8,512]{2,1,0:T(8,128)S(1)} collective-permute-done((f32[9,8,512]{2,1,0:T(8,128)}, f32[9,8,512]{2,1,0:T(8,128)S(1)}, u32[]{:S(2)}, u32[]{:S(2)}) %collective-permute-start.4) | collective-permute-done | bytes 147488 | tf_op jit(solution)/shard_map/ppermute | solution.py:92
  32.4 0.0 collective-permute-done.5.rest_5_
  32.4 0.0 collective-permute-done.6.rest_6_
  32.5 0.9 %contract.1 = (f32[3,8,512]{2,1,0:T(8,128)S(1)}, f32[3,8,128]{2,1,0:T(8,128)S(1)}, f32[3,8,128]{2,1,0:T(8,128)S(1)}, f32[3,3,8,8,512]{4,3,2,1,0:T(8,128)S(1)}) custom-call(s32[1]{0:T(128)} %bitcast.place_ref, f32[1,512]{1,0:T(1,128)S(1)} %get-tuple-element.64.mass_ref, f32[8,192]{1,0:T(8,128)S(1)} %copy-done.1, f32[9,8,512]{2,1,0:T(8,128)S(1)} %copy-done, ...), custom_call_target="tpu_custom_call" | custom-call | tf_op jit(solution)/shard_map/contract/pallas_call | solution.py:219
  33.4 0.8 %collective-permute-start.7 = (f32[3,8,128]{2,1,0:T(8,128)S(1)}, f32[3,8,128]{2,1,0:T(8,128)S(1)}, u32[]{:S(2)}, u32[]{:S(2)}) collective-permute-start(f32[3,8,128]{2,1,0:T(8,128)S(1)} %get-tuple-element.74), channel_id=1, source_target_pairs={{0,4},{1,5},{2,6},{3,7},{4,8},{5,9},{6,10},{7,11},{8,12},{9,13},{1... | collective-permute-start | bytes 36872 | tf_op jit(solution)/shard_map/ppermute | solution.py:631
  34.3 4.6 %collective-permute-start.8 = (f32[3,8,128]{2,1,0:T(8,128)S(1)}, f32[3,8,128]{2,1,0:T(8,128)S(1)}, u32[]{:S(2)}, u32[]{:S(2)}) collective-permute-start(f32[3,8,128]{2,1,0:T(8,128)S(1)} %get-tuple-element.75), channel_id=1, source_target_pairs={{4,0},{5,1},{6,2},{7,3},{8,4},{9,5},{10,6},{11,7},{12,8},{13,9},{1... | collective-permute-start | bytes 36872 | tf_op jit(solution)/shard_map/ppermute | solution.py:632
  38.8 1.6 %transform.1 = f32[8,6,8,512]{3,2,1,0:T(8,128)} custom-call(f32[3,3,8,8,512]{4,3,2,1,0:T(8,128)S(1)} %get-tuple-element.73.fields_ref, f32[1,512]{1,0:T(1,128)S(1)} %get-tuple-element.64.mass_ref, f32[128,192]{1,0:T(8,128)S(1)} %copy-done.9), custom_call_target="tpu_custom_call" | custom-call | flops 1000000000 | bytes 2000000 | tf_op jit(solution)/shard_map/transform/pallas_call | solution.py:260
  40.5 0.0 copy-start.5
  40.5 0.0 copy-start.6
  40.5 0.0 copy-start.8
  40.5 0.0 collective-permute-done.7.low_ref
  40.5 1.7 %collective-permute-done.8.up_ref = f32[3,8,128]{2,1,0:T(8,128)S(1)} collective-permute-done((f32[3,8,128]{2,1,0:T(8,128)S(1)}, f32[3,8,128]{2,1,0:T(8,128)S(1)}, u32[]{:S(2)}, u32[]{:S(2)}) %collective-permute-start.8) | collective-permute-done | bytes 12320 | tf_op jit(solution)/shard_map/ppermute | solution.py:632
  42.2 6.0 %all-to-all-start = ((f32[8,6,8,512]{3,2,1,0:T(8,128)}), f32[8,6,8,512]{3,2,1,0:T(8,128)S(1)}, u32[]{:S(2)}, u32[]{:S(2)}) async-start(f32[8,6,8,512]{3,2,1,0:T(8,128)} %transform.1), calls=%async_computation | async-start | bytes 1572864 | tf_op jit(solution)/shard_map/all_to_all | solution.py:635
  48.2 11.6 %neural.1 = f32[3,8,512]{2,1,0:T(8,128)S(1)} custom-call(f32[3,8,512]{2,1,0:T(8,128)S(1)} %get-tuple-element.77.c_ref, f32[3,8,128]{2,1,0:T(8,128)S(1)} %collective-permute-done.7.low_ref, f32[3,8,128]{2,1,0:T(8,128)S(1)} %collective-permute-done.8.up_ref, s32[32,512]{1,0:T(8,128)S(1)} %get-tuple-element.80.list_ref, ...), custom_call_target="tpu_custom_call" | custom-call | flops 12000000000 | bytes 4000000 | tf_op jit(solution)/shard_map/neural/pallas_call | solution.py:384
  59.7 2.9 %collective-permute-start.9 = (f32[1,3,8,512]{3,2,1,0:T(8,128)S(1)}, f32[1,3,8,512]{3,2,1,0:T(8,128)S(1)}, u32[]{:S(2)}, u32[]{:S(2)}) collective-permute-start(f32[1,3,8,512]{3,2,1,0:T(8,128)S(1)} %bitcast.18), channel_id=1, source_target_pairs={{0,16},{4,20},{8,24},{12,28},{16,0},{20,4},{24,8},{28,12},{1,17},{... | collective-permute-start | bytes 147464 | tf_op jit(solution)/shard_map/ppermute | solution.py:587
  62.7 6.6 %all-to-all-done.in_ref = f32[8,6,8,512]{3,2,1,0:T(8,128)S(1)} async-done(((f32[8,6,8,512]{3,2,1,0:T(8,128)}), f32[8,6,8,512]{3,2,1,0:T(8,128)S(1)}, u32[]{:S(2)}, u32[]{:S(2)}) %all-to-all-start) | async-done | bytes 786464 | tf_op jit(solution)/shard_map/all_to_all | solution.py:635
  69.2 0.8 assemble.1
  70.0 0.0 collective-permute-done.9
  70.0 0.1 collective-permute-start.10
  70.1 0.1 collective-permute-start.11
  70.2 1.7 %collective-permute-start.12 = (f32[3,8,128]{2,1,0:T(8,128)S(1)}, f32[3,8,128]{2,1,0:T(8,128)S(1)}, u32[]{:S(2)}, u32[]{:S(2)}) collective-permute-start(f32[3,8,128]{2,1,0:T(8,128)S(1)} %get-tuple-element.99), channel_id=1, source_target_pairs={{1,0},{2,1},{3,2},{0,3},{5,4},{6,5},{7,6},{4,7},{9,8},{10,9},{11,1... | collective-permute-start | bytes 36872 | tf_op jit(solution)/shard_map/ppermute | solution.py:647
  71.9 3.2 %pair_0.1.rest_0_ = f32[3,8,1536]{2,1,0:T(8,128)S(1)} custom-call(s32[3,4,4096]{2,1,0:T(4,128)S(1)} %get-tuple-element.91.words_ref, f32[3,8,4096]{2,1,0:T(8,128)S(1)} %get-tuple-element.87.fixed_ref, f32[8,128]{1,0:T(8,128)S(1)} %get-tuple-element.88.unit_ref, s32[32,4096]{1,0:T(8,128)S(1)} %get-tuple-element.89.list_ref), custom_call_target="tpu_custom_call" | custom-call | flops 3600000000 | bytes 2000000 | tf_op jit(solution)/shard_map/pair_0/pallas_call | solution.py:516
  75.2 0.0 collective-permute-done.10
  75.2 0.0 copy-start.11
  75.2 1.4 %collective-permute-start.13 = (f32[4,3,8,512]{3,2,1,0:T(8,128)S(1)}, f32[4,3,8,512]{3,2,1,0:T(8,128)S(1)}, u32[]{:S(2)}, u32[]{:S(2)}) collective-permute-start(f32[4,3,8,512]{3,2,1,0:T(8,128)S(1)} %pad_maximum_fusion.rest_2_), channel_id=1, source_target_pairs={{0,4},{4,0},{8,12},{12,8},{16,20},{20,16},{24,28},{28,24},{1,5},{5... | collective-permute-start | bytes 589832 | tf_op jit(solution)/shard_map/ppermute | solution.py:587
  76.6 0.0 collective-permute-done.11.rest_1_
  76.6 0.0 collective-permute-done.12.rest_2_
  76.6 6.3 %pair_12.1 = (f32[3,8,2560]{2,1,0:T(8,128)S(1)}, f32[3,8,128]{2,1,0:T(8,128)S(1)}) custom-call(s32[3,4,4096]{2,1,0:T(4,128)S(1)} %get-tuple-element.91.words_ref, f32[3,8,4096]{2,1,0:T(8,128)S(1)} %get-tuple-element.87.fixed_ref, f32[8,128]{1,0:T(8,128)S(1)} %get-tuple-element.88.unit_ref, s32[32,4096]{1,0:T(8,128)S(1)} %get-tuple-element.89.list_ref, ...), custom_call_target="tpu_custom_call" | custom-call | flops 6000000000 | bytes 2000000 | tf_op jit(solution)/shard_map/pair_12/pallas_call | solution.py:516
  82.9 0.0 collective-permute-done.13.rest_3_
  83.0 0.1 jit_solution_.3.coef_ref
  83.1 1.1 %finish.1 = (f32[3,8,4096]{2,1,0:T(8,128)}, f32[3,8,4096]{2,1,0:T(8,128)}) custom-call(s32[1]{0:T(128)} %bitcast.place_ref, f32[3,8,128]{2,1,0:T(8,128)S(1)} %get-tuple-element.93.first_ref, f32[8,8,8,128]{3,2,1,0:T(8,128)S(1)} %jit_solution_.3.coef_ref, f32[8,6,8,512]{3,2,1,0:T(8,128)S(1)} %all-to-all-done.in_ref, f32[3,8,1536]{2,1,0:T(8,128)S(1)} %pair_0.1.rest_0_, ...), custom_call_target="tpu_custom_call" | custom-call | tf_op jit(solution)/shard_map/finish/pallas_call | solution.py:569
  (19 shorter events, 0.1 us)
Async XLA Ops:
  0.6 18.7 %copy-start.10 = (bf16[128,128]{1,0:T(8,128)(2,1)S(1)}, bf16[128,128]{1,0:T(8,128)(2,1)}, u32[]{:S(2)}) copy-start(bf16[128,128]{1,0:T(8,128)(2,1)} %constant.14.clone.order_ref) | copy-start | bytes 98308
  0.6 18.7 %copy-start.3 = (s32[4096,32]{0,1:T(8,128)S(1)}, s32[4096,32]{0,1:T(8,128)}, u32[]{:S(2)}) copy-start(s32[4096,32]{0,1:T(8,128)} %param.20) | copy-start | bytes 1572868
  0.7 18.7 %copy-start.7 = (f32[4096]{0:T(1024)S(1)}, f32[4096]{0:T(1024)}, u32[]{:S(2)}) copy-start(f32[4096]{0:T(1024)} %param.19) | copy-start | bytes 49156
  0.7 18.7 %copy-start.2 = (bf16[1600,240]{0,1:T(8,128)(2,1)S(1)}, bf16[1600,240]{0,1:T(8,128)(2,1)}, u32[]{:S(2)}) copy-start(bf16[1600,240]{0,1:T(8,128)(2,1)} %param.22) | copy-start | bytes 2304004
  3.2 8.9 %collective-permute-start = (f32[9,8,512]{2,1,0:T(8,128)}, f32[9,8,512]{2,1,0:T(8,128)S(1)}, u32[]{:S(2)}, u32[]{:S(2)}) collective-permute-start(f32[9,8,512]{2,1,0:T(8,128)} %get-tuple-element.52), channel_id=1, source_target_pairs={{0,4},{4,0},{8,12},{12,8},{16,20},{20,16},{24,28},{28,24},{1,5},{5... | collective-permute-start | bytes 442376 | tf_op jit(solution)/shard_map/ppermute | solution.py:92
  6.2 12.2 %collective-permute-start.1 = (f32[9,8,512]{2,1,0:T(8,128)}, f32[9,8,512]{2,1,0:T(8,128)S(1)}, u32[]{:S(2)}, u32[]{:S(2)}) collective-permute-start(f32[9,8,512]{2,1,0:T(8,128)} %get-tuple-element.53), channel_id=1, source_target_pairs={{0,8},{4,12},{8,0},{12,4},{16,24},{20,28},{24,16},{28,20},{1,9},{5... | collective-permute-start | bytes 442376 | tf_op jit(solution)/shard_map/ppermute | solution.py:92
  7.8 12.9 %collective-permute-start.2 = (f32[9,8,512]{2,1,0:T(8,128)}, f32[9,8,512]{2,1,0:T(8,128)S(1)}, u32[]{:S(2)}, u32[]{:S(2)}) collective-permute-start(f32[9,8,512]{2,1,0:T(8,128)} %get-tuple-element.54), channel_id=1, source_target_pairs={{0,12},{4,8},{8,4},{12,0},{16,28},{20,24},{24,20},{28,16},{1,13},{... | collective-permute-start | bytes 442376 | tf_op jit(solution)/shard_map/ppermute | solution.py:92
  7.8 13.0 %collective-permute-start.3 = (f32[9,8,512]{2,1,0:T(8,128)}, f32[9,8,512]{2,1,0:T(8,128)S(1)}, u32[]{:S(2)}, u32[]{:S(2)}) collective-permute-start(f32[9,8,512]{2,1,0:T(8,128)} %get-tuple-element.55), channel_id=1, source_target_pairs={{0,16},{4,20},{8,24},{12,28},{16,0},{20,4},{24,8},{28,12},{1,17},{... | collective-permute-start | bytes 442376 | tf_op jit(solution)/shard_map/ppermute | solution.py:92
  10.8 21.7 %collective-permute-start.4 = (f32[9,8,512]{2,1,0:T(8,128)}, f32[9,8,512]{2,1,0:T(8,128)S(1)}, u32[]{:S(2)}, u32[]{:S(2)}) collective-permute-start(f32[9,8,512]{2,1,0:T(8,128)} %get-tuple-element.56), channel_id=1, source_target_pairs={{0,20},{4,16},{8,28},{12,24},{16,4},{20,0},{24,12},{28,8},{1,21},{... | collective-permute-start | bytes 442376 | tf_op jit(solution)/shard_map/ppermute | solution.py:92
  12.0 20.4 %collective-permute-start.5 = (f32[9,8,512]{2,1,0:T(8,128)}, f32[9,8,512]{2,1,0:T(8,128)S(1)}, u32[]{:S(2)}, u32[]{:S(2)}) collective-permute-start(f32[9,8,512]{2,1,0:T(8,128)} %get-tuple-element.57), channel_id=1, source_target_pairs={{0,24},{4,28},{8,16},{12,20},{16,8},{20,12},{24,0},{28,4},{1,25},{... | collective-permute-start | bytes 442376 | tf_op jit(solution)/shard_map/ppermute | solution.py:92
  18.4 14.1 %collective-permute-start.6 = (f32[9,8,512]{2,1,0:T(8,128)}, f32[9,8,512]{2,1,0:T(8,128)S(1)}, u32[]{:S(2)}, u32[]{:S(2)}) collective-permute-start(f32[9,8,512]{2,1,0:T(8,128)} %get-tuple-element.58), channel_id=1, source_target_pairs={{0,28},{4,24},{8,20},{12,16},{16,12},{20,8},{24,4},{28,0},{1,29},{... | collective-permute-start | bytes 442376 | tf_op jit(solution)/shard_map/ppermute | solution.py:92
  19.3 1.0 %copy-start.4 = (bf16[128,1600]{0,1:T(8,128)(2,1)S(1)}, bf16[128,1600]{0,1:T(8,128)(2,1)}, u32[]{:S(2)}) copy-start(bf16[128,1600]{0,1:T(8,128)(2,1)} %param.21) | copy-start | bytes 1228804
  20.3 12.1 %copy-start = (f32[9,8,512]{2,1,0:T(8,128)S(1)}, f32[9,8,512]{2,1,0:T(8,128)}, u32[]{:S(2)}) copy-start(f32[9,8,512]{2,1,0:T(8,128)} %get-tuple-element.65.own_ref) | copy-start | bytes 442372
  20.3 12.1 %copy-start.1 = (f32[8,192]{1,0:T(8,128)S(1)}, f32[8,192]{1,0:T(8,128)}, u32[]{:S(2)}) copy-start(f32[8,192]{1,0:T(8,128)} %constant.15.clone.table_ref) | copy-start | bytes 18436
  20.7 18.1 %copy-start.9 = (f32[128,192]{1,0:T(8,128)S(1)}, f32[128,192]{1,0:T(8,128)}, u32[]{:S(2)}) copy-start(f32[128,192]{1,0:T(8,128)} %constant.16.clone.table_ref) | copy-start | bytes 294916
  33.4 7.1 %collective-permute-start.7 = (f32[3,8,128]{2,1,0:T(8,128)S(1)}, f32[3,8,128]{2,1,0:T(8,128)S(1)}, u32[]{:S(2)}, u32[]{:S(2)}) collective-permute-start(f32[3,8,128]{2,1,0:T(8,128)S(1)} %get-tuple-element.74), channel_id=1, source_target_pairs={{0,4},{1,5},{2,6},{3,7},{4,8},{5,9},{6,10},{7,11},{8,12},{9,13},{1... | collective-permute-start | bytes 36872 | tf_op jit(solution)/shard_map/ppermute | solution.py:631
  34.3 7.9 %collective-permute-start.8 = (f32[3,8,128]{2,1,0:T(8,128)S(1)}, f32[3,8,128]{2,1,0:T(8,128)S(1)}, u32[]{:S(2)}, u32[]{:S(2)}) collective-permute-start(f32[3,8,128]{2,1,0:T(8,128)S(1)} %get-tuple-element.75), channel_id=1, source_target_pairs={{4,0},{5,1},{6,2},{7,3},{8,4},{9,5},{10,6},{11,7},{12,8},{13,9},{1... | collective-permute-start | bytes 36872 | tf_op jit(solution)/shard_map/ppermute | solution.py:632
  40.5 7.7 %copy-start.5 = (bf16[240,240]{1,0:T(8,128)(2,1)S(1)}, bf16[240,240]{1,0:T(8,128)(2,1)}, u32[]{:S(2)}) copy-start(bf16[240,240]{1,0:T(8,128)(2,1)} %w2.1) | copy-start | bytes 345604
  40.5 7.7 %copy-start.6 = (bf16[240,240]{1,0:T(8,128)(2,1)S(1)}, bf16[240,240]{1,0:T(8,128)(2,1)}, u32[]{:S(2)}) copy-start(bf16[240,240]{1,0:T(8,128)(2,1)} %w3.1) | copy-start | bytes 345604
  40.5 7.7 %copy-start.8 = (bf16[240,3]{0,1:T(4,128)(2,1)S(1)}, bf16[240,3]{0,1:T(4,128)(2,1)}, u32[]{:S(2)}) copy-start(bf16[240,3]{0,1:T(4,128)(2,1)} %param.25) | copy-start | bytes 4324
  42.2 27.1 %all-to-all-start = ((f32[8,6,8,512]{3,2,1,0:T(8,128)}), f32[8,6,8,512]{3,2,1,0:T(8,128)S(1)}, u32[]{:S(2)}, u32[]{:S(2)}) async-start(f32[8,6,8,512]{3,2,1,0:T(8,128)} %transform.1), calls=%async_computation | async-start | bytes 1572864 | tf_op jit(solution)/shard_map/all_to_all | solution.py:635
  59.7 10.3 %collective-permute-start.9 = (f32[1,3,8,512]{3,2,1,0:T(8,128)S(1)}, f32[1,3,8,512]{3,2,1,0:T(8,128)S(1)}, u32[]{:S(2)}, u32[]{:S(2)}) collective-permute-start(f32[1,3,8,512]{3,2,1,0:T(8,128)S(1)} %bitcast.18), channel_id=1, source_target_pairs={{0,16},{4,20},{8,24},{12,28},{16,0},{20,4},{24,8},{28,12},{1,17},{... | collective-permute-start | bytes 147464 | tf_op jit(solution)/shard_map/ppermute | solution.py:587
  70.0 5.1 %collective-permute-start.10 = (f32[2,3,8,512]{3,2,1,0:T(8,128)S(1)}, f32[2,3,8,512]{3,2,1,0:T(8,128)S(1)}, u32[]{:S(2)}, u32[]{:S(2)}) collective-permute-start(f32[2,3,8,512]{3,2,1,0:T(8,128)S(1)} %pad_maximum_fusion.1), channel_id=1, source_target_pairs={{0,8},{4,12},{8,0},{12,4},{16,24},{20,28},{24,16},{28,20},{1,9},{5... | collective-permute-start | bytes 294920 | tf_op jit(solution)/shard_map/ppermute | solution.py:587
  70.1 6.5 %collective-permute-start.11 = (f32[3,8,128]{2,1,0:T(8,128)S(1)}, f32[3,8,128]{2,1,0:T(8,128)S(1)}, u32[]{:S(2)}, u32[]{:S(2)}) collective-permute-start(f32[3,8,128]{2,1,0:T(8,128)S(1)} %get-tuple-element.100), channel_id=1, source_target_pairs={{0,1},{1,2},{2,3},{3,0},{4,5},{5,6},{6,7},{7,4},{8,9},{9,10},{10,1... | collective-permute-start | bytes 36872 | tf_op jit(solution)/shard_map/ppermute | solution.py:646
  70.2 6.4 %collective-permute-start.12 = (f32[3,8,128]{2,1,0:T(8,128)S(1)}, f32[3,8,128]{2,1,0:T(8,128)S(1)}, u32[]{:S(2)}, u32[]{:S(2)}) collective-permute-start(f32[3,8,128]{2,1,0:T(8,128)S(1)} %get-tuple-element.99), channel_id=1, source_target_pairs={{1,0},{2,1},{3,2},{0,3},{5,4},{6,5},{7,6},{4,7},{9,8},{10,9},{11,1... | collective-permute-start | bytes 36872 | tf_op jit(solution)/shard_map/ppermute | solution.py:647
  75.2 7.8 %copy-start.11 = (f32[8,8,8]{2,1,0:T(8,128)S(1)}, f32[8,8,8]{2,1,0:T(8,128)}, u32[]{:S(2)}) copy-start(f32[8,8,8]{2,1,0:T(8,128)} %constant.17.clone) | copy-start | bytes 6148
  75.2 7.7 %collective-permute-start.13 = (f32[4,3,8,512]{3,2,1,0:T(8,128)S(1)}, f32[4,3,8,512]{3,2,1,0:T(8,128)S(1)}, u32[]{:S(2)}, u32[]{:S(2)}) collective-permute-start(f32[4,3,8,512]{3,2,1,0:T(8,128)S(1)} %pad_maximum_fusion.rest_2_), channel_id=1, source_target_pairs={{0,4},{4,0},{8,12},{12,8},{16,20},{20,16},{24,28},{28,24},{1,5},{5... | collective-permute-start | bytes 589832 | tf_op jit(solution)/shard_map/ppermute | solution.py:587
